TPU v7x, 32 devices: a whole 2x2x4 slice. The times are simulated.
32 devices in a mesh: dp: 16 (over z, y, x), tensor: 2 (over core).
Axes of the slice: x: 2, y: 2, z: 4, core: 2. Of those that a mesh axis runs over, the one named last changes fastest.
Arguments:
- images: bfloat16 [16, 584, 1024], P('dp'), may hold values from -6 to 6
- image_mask: int32 [16], P('dp'), may hold values 0 or 1
- cotangent: bfloat16 [16, 584, 1024], P('dp'), may hold values from -6 to 6
- ln1_gain: bfloat16 [1024], replicated, may hold values from 0.5 to 1.5
- ln1_bias: bfloat16 [1024], replicated, may hold values from -1.25 to 1.25
- w_qkv: bfloat16 [1024, 3, 1024], P(None, None, 'tensor'), may hold values from -0.1875 to 0.1875
- qv_bias: bfloat16 [2, 1024], P(None, 'tensor'), may hold values from -1.75 to 1.75
- w_out: bfloat16 [1024, 1024], P('tensor'), may hold values from -3 to 3
- out_bias: bfloat16 [1024], replicated, may hold values from -1.75 to 1.75
- ln2_gain: bfloat16 [1024], replicated, may hold values from 0.5 to 1.5
- ln2_bias: bfloat16 [1024], replicated, may hold values from -1.25 to 1.25
- w_up: bfloat16 [1024, 4096], P(None, 'tensor'), may hold values from -0.1875 to 0.1875
- up_bias: bfloat16 [4096], P('tensor'), may hold values from -1.75 to 1.75
- w_down: bfloat16 [4096, 1024], P('tensor'), may hold values from -0.09375 to 0.09375
- down_bias: bfloat16 [1024], replicated, may hold values from -1.75 to 1.75
Outputs:
- block_output: bfloat16 [16, 584, 1024], P('dp')
- images_grad: bfloat16 [16, 584, 1024], P('dp')
- ln1_gain_grad: float32 [1024], replicated
- ln1_bias_grad: float32 [1024], replicated
- w_qkv_grad: float32 [1024, 3, 1024], P(None, None, 'tensor')
- qv_bias_grad: float32 [2, 1024], P(None, 'tensor')
- w_out_grad: float32 [1024, 1024], P('tensor')
- out_bias_grad: float32 [1024], replicated
- ln2_gain_grad: float32 [1024], replicated
- ln2_bias_grad: float32 [1024], replicated
- w_up_grad: float32 [1024, 4096], P(None, 'tensor')
- up_bias_grad: float32 [4096], P('tensor')
- w_down_grad: float32 [4096, 1024], P('tensor')
- down_bias_grad: float32 [1024], replicated
All inputs are finite; a program needn't handle non-finite values. No bound on the sum of `image_mask` on one device may be relied on, other than what follows from the above.
Results may differ from a plain program's by a relative error of at most 0.017.
Values may be sent and summed in bfloat16 or wider, within the bound.
No kernel may reach another device: no remote copies, remote signals or barrier semaphores. Data moves between devices by JAX's collectives and lax.ppermute only.
A program may use at most 192 MiB of HBM per device.

v0:
```python
import jax
import jax.numpy as jnp
from jax import lax
from jax.experimental import pallas as pl
from jax.experimental.pallas import tpu as pltpu
from jax.sharding import PartitionSpec as P

HD = 64
VALID = 577
EPS = 1e-06
BF = jnp.bfloat16
F32 = jnp.float32


def stats(values):
    mean = jnp.mean(values, axis=-1, keepdims=True)
    centred = values - mean
    spread = jnp.mean(centred * centred, axis=-1, keepdims=True)
    inv = lax.rsqrt(spread + EPS)
    return centred * inv, inv


def norm_back(unit, inv, gain, grad):
    scaled = grad * gain
    mean_a = jnp.mean(scaled, axis=-1, keepdims=True)
    mean_b = jnp.mean(scaled * unit, axis=-1, keepdims=True)
    return inv * (scaled - mean_a - unit * mean_b)


def inner_rows(left, right):
    return lax.dot_general(
        left, right, (((0,), (0,)), ((), ())), preferred_element_type=F32
    )


def times_back(left, weight):
    return lax.dot_general(
        left, weight, (((1,), (1,)), ((), ())), preferred_element_type=F32
    )


def score_block(query, keyset):
    raw = jnp.einsum("qhd,khd->hqk", query, keyset, preferred_element_type=F32)
    live = jnp.arange(raw.shape[-1]) < VALID
    return jnp.where(live, raw * HD ** (-0.5), -1e30)


def attend_forward(query, keyset, valueset):
    scores = score_block(query, keyset)
    peak = jnp.max(scores, axis=-1, keepdims=True)
    expo = jnp.exp(scores - peak)
    total = jnp.sum(expo, axis=-1, keepdims=True)
    probs = (expo / total).astype(BF)
    mixed = jnp.einsum("hqk,khd->qhd", probs, valueset, preferred_element_type=F32)
    return mixed.astype(BF), peak[..., 0] + jnp.log(total[..., 0])


def attend_backward(query, keyset, valueset, grad_mixed, logsum):
    scores = score_block(query, keyset)
    probs = jnp.exp(scores - logsum[..., None])
    grad_probs = jnp.einsum("qhd,khd->hqk", grad_mixed, valueset, preferred_element_type=F32)
    delta = jnp.sum(probs * grad_probs, axis=-1, keepdims=True)
    grad_scores = (probs * (grad_probs - delta) * HD ** (-0.5)).astype(BF)
    low_probs = probs.astype(BF)
    grad_value = jnp.einsum("hqk,qhd->khd", low_probs, grad_mixed, preferred_element_type=F32)
    grad_query = jnp.einsum("hqk,khd->qhd", grad_scores, keyset, preferred_element_type=F32)
    grad_key = jnp.einsum("hqk,qhd->khd", grad_scores, query, preferred_element_type=F32)
    return jnp.stack([grad_query, grad_key, grad_value], axis=1).astype(BF)


def swap_sum(part):
    if lax.axis_size("tensor") == 2:
        other = lax.ppermute(part, "tensor", [(0, 1), (1, 0)])
        return part.astype(F32) + other.astype(F32)
    return lax.psum(part.astype(F32), "tensor")


def xor_pairs(bit):
    return [(i, i ^ bit) for i in range(lax.axis_size("dp"))]


def bits_of():
    count = lax.axis_size("dp")
    bits = []
    while count > 1:
        if count % 2:
            raise ValueError("dp")
        bits.append(1 << len(bits))
        count //= 2
    return bits


def sum_small(vector):
    for bit in bits_of():
        vector = vector + lax.ppermute(vector, "dp", xor_pairs(bit))
    return vector


def cut_thirds(rows, turn):
    unit = 128
    whole = rows // unit
    base = whole // 3
    counts = [base + (1 if (i - turn) % 3 < whole % 3 else 0) for i in range(3)]
    return [c * unit for c in counts]


def sum_over_dp(matrix, turn):
    bits = bits_of()
    index = lax.axis_index("dp")
    halving = bits[: min(3, len(bits) - 1)]
    swaps = bits[len(halving) :]
    pieces, orders, start = [], [], 0
    for lane, rows in enumerate(cut_thirds(matrix.shape[0], turn)):
        if rows == 0:
            continue
        pieces.append(lax.slice_in_dim(matrix, start, start + rows, axis=0))
        turned = lane % len(halving)
        orders.append(halving[turned:] + halving[:turned])
        start += rows
    for step in range(len(halving)):
        for lane in range(len(pieces)):
            piece, bit = pieces[lane], orders[lane][step]
            half = piece.shape[0] // 2
            side = (index // bit) & 1
            kept = lax.dynamic_slice_in_dim(piece, side * half, half, 0)
            sent = lax.dynamic_slice_in_dim(piece, (1 - side) * half, half, 0)
            pieces[lane] = kept + lax.ppermute(sent, "dp", xor_pairs(bit))
    for bit in swaps:
        for lane in range(len(pieces)):
            pieces[lane] = pieces[lane] + lax.ppermute(pieces[lane], "dp", xor_pairs(bit))
    for step in reversed(range(len(halving))):
        for lane in range(len(pieces)):
            piece, bit = pieces[lane], orders[lane][step]
            other = lax.ppermute(piece, "dp", xor_pairs(bit))
            side = (index // bit) & 1
            pieces[lane] = jnp.where(
                side == 0,
                jnp.concatenate([piece, other], axis=0),
                jnp.concatenate([other, piece], axis=0),
            )
    return jnp.concatenate(pieces, axis=0).astype(F32)


def shards_any(
    images,
    image_mask,
    cotangent,
    ln1_gain,
    ln1_bias,
    w_qkv,
    qv_bias,
    w_out,
    out_bias,
    ln2_gain,
    ln2_bias,
    w_up,
    up_bias,
    w_down,
    down_bias,
):
    count, seq, width = images.shape
    rows = count * seq
    local = w_qkv.shape[2]
    heads = local // HD
    gain1 = ln1_gain.astype(F32)
    gain2 = ln2_gain.astype(F32)
    inputs = images.reshape(rows, width).astype(F32)
    keep = image_mask.astype(BF)[:, None, None]
    grad_out = (cotangent * keep).reshape(rows, width)
    w_qkv_flat = w_qkv.reshape(width, 3 * local)
    bias_row = jnp.concatenate([qv_bias[0], jnp.zeros_like(qv_bias[0]), qv_bias[1]]).astype(F32)

    unit1, inv1 = stats(inputs)
    normed1 = (unit1 * gain1 + ln1_bias.astype(F32)).astype(BF)
    qkv = (jnp.dot(normed1, w_qkv_flat, preferred_element_type=F32) + bias_row).astype(BF)
    split = qkv.reshape(count, seq, 3, heads, HD)
    attended = [attend_forward(split[i, :, 0], split[i, :, 1], split[i, :, 2]) for i in range(count)]
    mixed = jnp.concatenate([a[0] for a in attended], axis=0).reshape(rows, local)
    attn = swap_sum(jnp.dot(mixed, w_out, preferred_element_type=F32).astype(BF))
    grad_act = times_back(grad_out, w_down)
    resid = inputs + attn + out_bias.astype(F32)
    unit2, inv2 = stats(resid)
    normed2 = (unit2 * gain2 + ln2_bias.astype(F32)).astype(BF)
    pre = jnp.dot(normed2, w_up, preferred_element_type=F32) + up_bias.astype(F32)
    cdf = 0.5 * (1.0 + lax.erf(pre * (0.5**0.5)))
    act = (pre * cdf).astype(BF)
    slope = cdf + pre * jnp.exp(-0.5 * pre * pre) * ((0.5 / jnp.pi) ** 0.5)
    grad_pre = (grad_act * slope).astype(BF)
    grad_wdown = inner_rows(act, grad_out).astype(BF)
    summed_wdown = sum_over_dp(grad_wdown, 0)
    grad_wup = inner_rows(normed2, grad_pre).astype(BF)
    summed_wup = sum_over_dp(grad_wup, 1)
    grad_normed2 = swap_sum(times_back(grad_pre, w_up).astype(BF))
    mlp = swap_sum(jnp.dot(act, w_down, preferred_element_type=F32).astype(BF))
    block_output = (resid + mlp + down_bias.astype(F32)).astype(BF).reshape(images.shape)
    grad_resid = grad_out.astype(F32) + norm_back(unit2, inv2, gain2, grad_normed2)
    resid_low = grad_resid.astype(BF)
    grad_wout = inner_rows(mixed, resid_low).astype(BF)
    summed_wout = sum_over_dp(grad_wout, 2)
    grad_mixed = times_back(resid_low, w_out).astype(BF).reshape(count, seq, heads, HD)
    grad_qkv = jnp.concatenate(
        [
            attend_backward(split[i, :, 0], split[i, :, 1], split[i, :, 2], grad_mixed[i], attended[i][1])
            for i in range(count)
        ],
        axis=0,
    ).reshape(rows, 3 * local)
    grad_wqkv = inner_rows(normed1, grad_qkv).astype(BF)
    summed_wqkv = sum_over_dp(grad_wqkv, 0).reshape(width, 3, local)
    bias_sums = jnp.sum(grad_qkv.astype(F32), axis=0)
    grad_normed1 = swap_sum(times_back(grad_qkv, w_qkv_flat).astype(BF))
    images_grad = (
        (grad_resid + norm_back(unit1, inv1, gain1, grad_normed1)).astype(BF).reshape(images.shape)
    )

    small = [
        jnp.sum(grad_normed1 * unit1, axis=0),
        jnp.sum(grad_normed1, axis=0),
        jnp.sum(grad_resid, axis=0),
        jnp.sum(grad_normed2 * unit2, axis=0),
        jnp.sum(grad_normed2, axis=0),
        jnp.sum(grad_out.astype(F32), axis=0),
        jnp.sum(grad_pre.astype(F32), axis=0),
        bias_sums[:local],
        bias_sums[2 * local :],
    ]
    flat = jnp.concatenate(small)
    length = flat.shape[0]
    padded = -(-length // 1024) * 1024
    flat = sum_small(jnp.pad(flat, (0, padded - length)).reshape(padded // 128, 128)).reshape(-1)
    out, at = [], 0
    for part in small:
        out.append(flat[at : at + part.shape[0]])
        at += part.shape[0]
    return (
        block_output,
        images_grad,
        out[0],
        out[1],
        summed_wqkv,
        jnp.stack([out[7], out[8]]),
        summed_wout,
        out[2],
        out[3],
        out[4],
        summed_wup,
        out[6],
        summed_wdown,
        out[5],
    )


CHUNKS = 2
ANY = pl.BlockSpec(memory_space=pl.ANY)
HBM = pl.BlockSpec(memory_space=pltpu.HBM)
VM = pl.BlockSpec(memory_space=pltpu.VMEM)
MIB = 1024 * 1024


def shape_of(shape, dtype):
    return jax.ShapeDtypeStruct(shape, dtype)


def nn(left, right):
    return jnp.dot(left, right, preferred_element_type=F32)


def normal_unit(values):
    mean = jnp.mean(values, axis=-1, keepdims=True)
    centred = values - mean
    spread = jnp.mean(centred * centred, axis=-1, keepdims=True)
    inv = lax.rsqrt(spread + EPS)
    return centred * inv, inv


def row_of(ref):
    return ref[...].astype(F32).reshape(1, ref.shape[0])


def side_of(where_ref, bits):
    bit = bits[0] if bits[0] == bits[1] else jnp.where(where_ref[1] == 0, bits[0], bits[1])
    return (where_ref[0] >> bit) & 1


class Chain:
    def __init__(self):
        self.last = None

    def __call__(
        self, body, args, in_specs, outs, out_specs, scratch=(), grid=(), vmem=40, aliases=None, name=None, prefetch=0, cost=0.001
    ):
        args, in_specs, run = list(args), list(in_specs), body
        if self.last is not None:
            spot = len(args)

            def run(*refs):
                body(*refs[:spot], *refs[spot + 1 :])

            args.append(self.last)
            in_specs.append(ANY)
        spec = pltpu.PrefetchScalarGridSpec(
            num_scalar_prefetch=prefetch,
            grid=grid,
            in_specs=in_specs,
            out_specs=out_specs,
            scratch_shapes=list(scratch),
        )
        made = pl.pallas_call(
            run,
            out_shape=outs,
            grid_spec=spec,
            input_output_aliases=aliases or {},
            compiler_params=pltpu.CompilerParams(vmem_limit_bytes=vmem * MIB),
            cost_estimate=pl.CostEstimate(flops=0, bytes_accessed=int(cost * 3e6), transcendentals=0),
            name=name,
        )(*args)
        self.last = made[0] if isinstance(made, (tuple, list)) else made
        return made


def row_chunks(rows):
    units, parts = rows // 16, CHUNKS
    cuts = [16 * (units * i // parts) for i in range(parts)] + [rows]
    return [(cuts[i], cuts[i + 1] - cuts[i]) for i in range(parts)]


def lane_halves():
    return lax.broadcasted_iota(jnp.int32, (1, 2 * HD), 1) < HD


def key_mask(length):
    return jnp.where(lax.broadcasted_iota(jnp.int32, (1, length), 1) < VALID, 0.0, -1e30)


def copier(sems):
    count = [0]

    def copy(source, target):
        made = pltpu.make_async_copy(source, target, sems.at[count[0]])
        count[0] += 1
        made.start()
        return made

    return copy


def attend_kernel(
    mask_ref, g_ref, s_ref, b_ref, x_ref, w_ref, wo_ref, cot_ref, wd_ref,
    part_ref, q_ref, k_ref, v_ref, mixed_ref, n1_ref, lse_ref, ga_ref, go_ref, bd_ref,
    x_b, w_b, wo_b, cot_b, wd_b, part_b, q_b, k_b, v_b, mixed_b, n1_b, lse_b, ga_b, go_b, sems,
):
    rows, width = x_ref.shape
    padded, local = q_ref.shape
    pairs = local // 128
    deep = wd_ref.shape[0] // pairs
    copy = copier(sems)
    get_x = copy(x_ref, x_b)
    get_w = [copy(w_ref.at[c], w_b.at[c]) for c in range(3)]
    get_cot = copy(cot_ref, cot_b)
    get_wd = [copy(wd_ref.at[pl.ds(i * deep, deep)], wd_b.at[i]) for i in range(pairs)]
    get_wo = copy(wo_ref, wo_b)
    puts = []
    get_x.wait()
    unit, _ = normal_unit(x_b[...].astype(F32))
    normed = unit * row_of(g_ref) + row_of(s_ref)
    n1_b[...] = jnp.concatenate([normed, jnp.zeros((padded - rows, width), F32)], axis=0).astype(BF)
    puts.append(copy(n1_b, n1_ref))
    lse_b[...] = jnp.zeros(lse_b.shape, F32)
    live = lax.broadcasted_iota(jnp.int32, (padded, 1), 0) < rows
    for c, (buf, ref, scale) in enumerate(((q_b, q_ref, HD ** (-0.5)), (k_b, k_ref, 1.0), (v_b, v_ref, 1.0))):
        get_w[c].wait()
        for at in range(0, local, 256):
            made = nn(n1_b[...], w_b[c, :, at : at + 256])
            if c != 1:
                made = made + b_ref[c // 2 : c // 2 + 1, at : at + 256].astype(F32)
            made = jnp.where(live, made, 0.0).astype(BF)
            buf[:, at : at + 256] = made * jnp.asarray(scale, BF)
        puts.append(copy(buf, ref))
    get_cot.wait()
    masked = cot_b[...].astype(F32) * mask_ref[0].astype(F32)
    go_b[...] = masked.astype(BF)
    puts.append(copy(go_b, go_ref))
    bd_ref[...] = jnp.sum(masked, axis=0, keepdims=True)
    for get in get_wd:
        get.wait()
    mask = key_mask(padded)
    first = lane_halves()
    lane = lax.broadcasted_iota(jnp.int32, (1, 128), 1)

    def pair(p, carry):
        cols = pl.ds(pl.multiple_of(p * 128, 128), 128)
        keys, vals = k_b[:, cols], v_b[:, cols]
        query = q_b[:, cols]
        zero, ones = jnp.zeros_like(keys), jnp.ones_like(vals)
        own_k = (jnp.where(first, keys, zero), jnp.where(first, zero, keys))
        own_v = (jnp.where(first, vals, ones), jnp.where(first, ones, vals))
        ga_b[:, pl.ds(pl.multiple_of(p * deep, deep), deep)] = times_back(go_b[...], wd_b[p]).astype(BF)
        outs = []
        logs = lse_b[...]
        for h in range(2):
            scores = times_back(query, own_k[h]) + mask
            peak = jnp.max(scores, axis=-1, keepdims=True)
            made = nn(jnp.exp(scores - peak).astype(BF), own_v[h])
            total = made[:, HD : HD + 1] if h == 0 else made[:, 0:1]
            outs.append(made * (1.0 / total))
            logs = jnp.where(lane == 2 * p + h, peak + jnp.log(total), logs)
        lse_b[...] = logs
        mixed_b[:, cols] = jnp.where(first, outs[0], outs[1]).astype(BF)
        return carry

    lax.fori_loop(0, pairs, pair, 0)
    puts += [copy(ga_b, ga_ref), copy(mixed_b, mixed_ref), copy(lse_b, lse_ref)]
    get_wo.wait()
    for at in range(0, width, 256):
        made = nn(mixed_b[...], wo_b[:, at : at + 256])
        part_b[:, at : at + 256] = made[:rows].astype(BF)
    puts.append(copy(part_b, part_ref))
    for put in puts:
        put.wait()


def attend(chain, mask, gain, shift, bias, x, w3, w_out, cot, w_down):
    rows, width = x.shape
    local = w3.shape[2]
    hidden = w_down.shape[0]
    padded = -(-rows // 16) * 16
    pairs = local // 128
    slab = ((rows, width), BF)
    wide = ((padded, local), BF)
    outs = (slab, wide, wide, wide, wide, ((padded, width), BF), ((padded, 128), F32), ((rows, hidden), BF), slab)
    held = (slab, ((3, width, local), BF), ((local, width), BF), slab, ((pairs, hidden // pairs, width), BF)) + outs
    return chain(
        attend_kernel,
        (mask, gain, shift, bias, x, w3, w_out, cot, w_down),
        [VM] * 3 + [HBM] * 5,
        tuple(shape_of(*out) for out in outs) + (shape_of((1, width), F32),),
        (HBM,) * len(outs) + (VM,),
        [pltpu.VMEM(*hold) for hold in held] + [pltpu.SemaphoreType.DMA((7 + pairs + len(outs),))],
        name="attend",
        vmem=60,
        prefetch=1,
    )


def gelu_pair(pre):
    bell = jnp.exp(-0.5 * pre * pre)
    near = 1.0 / (1.0 + (0.3275911 * 0.5**0.5) * jnp.abs(pre))
    poly = near * (
        0.254829592 + near * (-0.284496736 + near * (1.421413741 + near * (-1.453152027 + near * 1.061405429)))
    )
    tail = 0.5 * poly * bell
    cdf = jnp.where(pre < 0, tail, 1.0 - tail)
    return cdf, cdf + pre * bell * ((0.5 / jnp.pi) ** 0.5)


def feed_kernel(
    where_ref, ob_ref, g_ref, s_ref, ub_ref, x_ref, pa_ref, pb_ref, go_ref, wu_ref, ga_ref,
    act_ref, gn_ref, ds0_ref, ds1_ref, dk0_ref, dk1_ref, us0_ref, us1_ref, uk0_ref, uk1_ref, bu_ref,
    x_b, pa_b, pb_b, go_b, wu_b, ga_b, act_b, n2_b, down_b, up_b, gn_b, total, bias, sems, *, bits,
):
    rows, width = x_ref.shape
    hidden = wu_ref.shape[1]
    size = hidden // 4
    tall = width // 4
    sides = [side_of(where_ref, bit) for bit in bits]
    starts = [pl.multiple_of((2 * lane + (1 - sides[lane])) * size, size) for lane in range(2)]
    starts += [pl.multiple_of((2 * lane + sides[lane]) * size, size) for lane in range(2)]
    tops = [pl.multiple_of((2 * lane + (1 - sides[2 + lane])) * tall, tall) for lane in range(2)]
    tops += [pl.multiple_of((2 * lane + sides[2 + lane]) * tall, tall) for lane in range(2)]
    copy = copier(sems)
    gets = [copy(x_ref, x_b), copy(pa_ref, pa_b), copy(pb_ref, pb_b)]
    get_w, get_ga = [], []
    for c in range(4):
        get_w.append(copy(wu_ref.at[:, pl.ds(starts[c], size)], wu_b.at[c]))
        get_ga.append(copy(ga_ref.at[:, pl.ds(starts[c], size)], ga_b.at[c]))
        if c == 0:
            get_go = copy(go_ref, go_b)
    puts = []
    bias[...] = row_of(ub_ref)
    for get in gets:
        get.wait()
    resid = x_b[...].astype(F32) + (pa_b[...].astype(F32) + pb_b[...].astype(F32)) + row_of(ob_ref)
    unit, _ = normal_unit(resid)
    n2_b[...] = (unit * row_of(g_ref) + row_of(s_ref)).astype(BF)

    def front(c):
        get_w[c].wait()
        get_ga[c].wait()
        for at in range(0, size, 256):
            cols = pl.ds(pl.multiple_of(starts[c] + at, 256), 256)
            pre = nn(n2_b[...], wu_b[c, :, at : at + 256]) + bias[:, cols]
            cdf, slope = gelu_pair(pre)
            act_b[c, :, at : at + 256] = (pre * cdf).astype(BF)
            grad_pre = (ga_b[c, :, at : at + 256].astype(F32) * slope).astype(BF)
            ga_b[c, :, at : at + 256] = grad_pre
            bu_ref[:, cols] = jnp.sum(grad_pre.astype(F32), axis=0, keepdims=True)
        puts.append(copy(act_b.at[c], act_ref.at[:, pl.ds(starts[c], size)]))

    def back(c):
        if c == 0:
            get_go.wait()
        for at in range(0, width, 512):
            made = inner_rows(act_b[c], go_b[:, at : at + 512])
            down_b[c, :, at : at + 512] = made.astype(BF)
        puts.append(copy(down_b.at[c], (ds0_ref, ds1_ref, dk0_ref, dk1_ref)[c]))
        for piece in range(4):
            made = inner_rows(n2_b[:, pl.ds(tops[piece], tall)], ga_b[c])
            up_b[piece, :, pl.ds(starts[c], size)] = made.astype(BF)
        for at in range(0, width, 512):
            made = times_back(ga_b[c], wu_b[c, at : at + 512, :])
            if c:
                made = made + total[:, at : at + 512]
            if c < 3:
                total[:, at : at + 512] = made
            else:
                gn_b[:, at : at + 512] = made.astype(BF)

    for c in range(5):
        if c < 4:
            front(c)
        if c:
            back(c - 1)
    puts.append(copy(gn_b, gn_ref))
    for piece, ref in enumerate((us0_ref, us1_ref, uk0_ref, uk1_ref)):
        puts.append(copy(up_b.at[piece], ref))
    for put in puts:
        put.wait()


def feed(chain, where, bits, out_bias, gain, shift, up_bias, x, pa, pb, go, w_up, ga):
    rows, width = x.shape
    hidden = w_up.shape[1]

    def body(*refs):
        feed_kernel(*refs, bits=bits)

    slab = ((rows, width), BF)
    deep = ((4, rows, hidden // 4), BF)
    outs = (((rows, hidden), BF), slab) + (((hidden // 4, width), BF),) * 4 + (((width // 4, hidden), BF),) * 4
    held = (slab,) * 4 + (((4, width, hidden // 4), BF), deep, deep, slab, ((4, hidden // 4, width), BF))
    held += (((4, width // 4, hidden), BF), slab, ((rows, width), F32), ((1, hidden), F32))
    return chain(
        body,
        (where, out_bias, gain, shift, up_bias, x, pa, pb, go, w_up, ga),
        [VM] * 4 + [HBM] * 6,
        tuple(shape_of(*out) for out in outs) + (shape_of((1, hidden), F32),),
        (HBM,) * len(outs) + (VM,),
        [pltpu.VMEM(*hold) for hold in held] + [pltpu.SemaphoreType.DMA((12 + 4 + len(outs),))],
        name="feed",
        vmem=60,
        prefetch=1,
    )


def qkv_grad(chain, where, n1, grads, out_grad, bits, flip):
    width = n1.shape[1]
    local = grads.shape[1] // 3
    size = width // 4

    def body(where_ref, n1_ref, g_ref, o_ref, first_ref, second_ref):
        def product(ref, start):
            for i in range(4):
                made = inner_rows(n1_ref[:, i * size : (i + 1) * size], g_ref[:, pl.ds(start, local)])
                ref[i * size : (i + 1) * size, :] = made.astype(BF)

        product(first_ref, pl.multiple_of((side_of(where_ref, bits[0]) ^ flip) * local, local))
        which = side_of(where_ref, bits[1]) ^ flip

        @pl.when(which == 0)
        def _():
            product(second_ref, 2 * local)

        @pl.when(which == 1)
        def _():
            second_ref[...] = o_ref[...]

    return chain(
        body,
        (where, n1, grads, out_grad),
        [VM, VM, VM],
        (shape_of((width, local), BF),) * 2,
        (VM,) * 2,
        name="qkv_grad",
        prefetch=1,
    )


TILES = 4


def paired(own, other):
    return own[...].astype(F32) + other[...].astype(F32)


def down(chain, act, w_down):
    rows, hidden = act.shape
    width = w_down.shape[1]
    size = width // TILES
    deep = hidden // TILES

    def body(act_ref, w_ref, *rest):
        out_ref, w_buf, sems = rest
        copies = [
            pltpu.make_async_copy(w_ref.at[pl.ds(i * deep, deep)], w_buf.at[pl.ds(i * deep, deep)], sems.at[i])
            for i in range(TILES)
        ]
        for copy in copies:
            copy.start()
        for copy in copies:
            copy.wait()
        for i in range(TILES):
            out_ref[:, i * size : (i + 1) * size] = nn(act_ref[...], w_buf[:, i * size : (i + 1) * size]).astype(BF)

    return chain(
        body,
        (act, w_down),
        [VM, HBM],
        shape_of((rows, width), BF),
        VM,
        [pltpu.VMEM((hidden, width), BF), pltpu.SemaphoreType.DMA((TILES,))],
        name="down",
    )


def resid_back_kernel(
    x_ref, pa_ref, pb_ref, ob_ref, g_ref, ga_ref, gb_ref, go_ref, mixed_ref, wo_ref, gr_ref, gm_ref, sums_ref, og_ref, low
):
    rows, width = x_ref.shape
    padded, local = mixed_ref.shape
    resid = x_ref[...].astype(F32) + (pa_ref[...].astype(F32) + pb_ref[...].astype(F32)) + row_of(ob_ref)
    unit, inv = normal_unit(resid)
    grad = paired(ga_ref, gb_ref)
    total = go_ref[...].astype(F32) + norm_back(unit, inv, row_of(g_ref), grad)
    gr_ref[...] = total
    low[...] = jnp.concatenate([total, jnp.zeros((padded - rows, width), F32)], axis=0).astype(BF)
    sums_ref[...] = jnp.concatenate(
        [
            jnp.sum(total, axis=0, keepdims=True),
            jnp.sum(grad * unit, axis=0, keepdims=True),
            jnp.sum(grad, axis=0, keepdims=True),
            jnp.zeros((5, width), F32),
        ],
        axis=0,
    )
    for i in range(2):
        for at in range(0, width // 2, 256):
            start = i * width // 2 + at
            made = inner_rows(mixed_ref[...], low[:, start : start + 256])
            og_ref[i * local : (i + 1) * local, at : at + 256] = made.astype(BF)
    for at in range(0, local, 256):
        gm_ref[:, at : at + 256] = times_back(low[...], wo_ref[at : at + 256, :]).astype(BF)


def resid_back(chain, x, pa, pb, out_bias, gain, ga, gb, go, mixed, w_out):
    rows, width = x.shape
    padded, local = mixed.shape
    return chain(
        resid_back_kernel,
        (x, pa, pb, out_bias, gain, ga, gb, go, mixed, w_out),
        [VM] * 10,
        (
            shape_of((rows, width), F32),
            shape_of((padded, local), BF),
            shape_of((8, width), F32),
            shape_of((2 * local, width // 2), BF),
        ),
        (VM,) * 4,
        [pltpu.VMEM((padded, width), BF)],
        name="resid_back",
    )


def attend_back_kernel(q_ref, k_ref, v_ref, mixed_ref, gm_ref, lse_ref, out_ref, bias_ref, probs_s, slopes_s):
    padded, local = q_ref.shape
    mask = key_mask(padded)
    first = lane_halves()
    lane = lax.broadcasted_iota(jnp.int32, (1, 128), 1)

    def pair(p, carry):
        cols = pl.ds(pl.multiple_of(p * 128, 128), 128)
        keys, vals = k_ref[:, cols], v_ref[:, cols]
        zero = jnp.zeros_like(keys)
        own_k = (jnp.where(first, keys, zero), jnp.where(first, zero, keys))
        own_v = (jnp.where(first, vals, zero), jnp.where(first, zero, vals))
        for at, size in row_chunks(padded):
            query = q_ref[at : at + size, cols]
            grad = gm_ref[at : at + size, cols]
            both = grad.astype(F32) * mixed_ref[at : at + size, cols].astype(F32)
            logs = lse_ref[at : at + size, :]
            outs = []
            for h in range(2):
                own_lanes = first if h == 0 else jnp.logical_not(first)
                delta = jnp.sum(jnp.where(own_lanes, both, 0.0), axis=-1, keepdims=True)
                log = jnp.sum(jnp.where(lane == 2 * p + h, logs, 0.0), axis=-1, keepdims=True)
                probs = jnp.exp(times_back(query, own_k[h]) + mask - log)
                slope = (probs * (times_back(grad, own_v[h]) - delta)).astype(BF)
                probs_s[h, at : at + size, :] = probs.astype(BF)
                slopes_s[h, at : at + size, :] = slope
                outs.append(nn(slope, keys))
            out_ref[at : at + size, cols] = (jnp.where(first, outs[0], outs[1]) * HD ** (-0.5)).astype(BF)
        grad_t = gm_ref[:, cols].astype(F32).T.astype(BF)
        query_t = q_ref[:, cols].astype(F32).T.astype(BF)
        grad_k = [nn(query_t[HD * h : HD * h + HD], slopes_s[h]) for h in range(2)]
        grad_v = [nn(grad_t[HD * h : HD * h + HD], probs_s[h]) for h in range(2)]
        cols_k = pl.ds(pl.multiple_of(local + p * 128, 128), 128)
        cols_v = pl.ds(pl.multiple_of(2 * local + p * 128, 128), 128)
        out_ref[:, cols_k] = jnp.concatenate(grad_k, axis=0).T.astype(BF)
        out_ref[:, cols_v] = jnp.concatenate(grad_v, axis=0).T.astype(BF)
        return carry

    lax.fori_loop(0, local // 128, pair, 0)
    bias_ref[...] = jnp.sum(out_ref[...].astype(F32), axis=0, keepdims=True)


def attend_back(chain, q, k, v, mixed, gm, lse):
    padded, local = q.shape
    return chain(
        attend_back_kernel,
        (q, k, v, mixed, gm, lse),
        [VM] * 6,
        (shape_of((padded, 3 * local), BF), shape_of((1, 3 * local), F32)),
        (VM, VM),
        [pltpu.VMEM((2, padded, padded), BF), pltpu.VMEM((2, padded, padded), BF)],
        name="attend_back",
    )


def back_in(chain, grads, w3, rows):
    _, width, local = w3.shape
    size = width // TILES

    def body(g_ref, w_ref, *rest):
        out_ref, w_buf, sems = rest
        copies = [
            pltpu.make_async_copy(w_ref.at[:, pl.ds(i * size, size)], w_buf.at[i], sems.at[i]) for i in range(TILES)
        ]
        for copy in copies:
            copy.start()
        for i in range(TILES):
            copies[i].wait()
            total = times_back(g_ref[:, :local], w_buf[i, 0])
            for c in range(1, 3):
                total += times_back(g_ref[:, c * local : (c + 1) * local], w_buf[i, c])
            out_ref[:, i * size : (i + 1) * size] = total[:rows].astype(BF)

    return chain(
        body,
        (grads, w3),
        [VM, HBM],
        shape_of((rows, width), BF),
        VM,
        [pltpu.VMEM((TILES, 3, size, local), BF), pltpu.SemaphoreType.DMA((TILES,))],
        name="back_in",
    )


def images_back_kernel(x_ref, g_ref, gr_ref, ga_ref, gb_ref, bd_ref, bu_ref, s2_ref, bq_ref, out_ref, pack_ref):
    unit, inv = normal_unit(x_ref[...].astype(F32))
    grad = paired(ga_ref, gb_ref)
    out_ref[...] = (gr_ref[...] + norm_back(unit, inv, row_of(g_ref), grad)).astype(BF)
    width = x_ref.shape[1]
    hidden = bu_ref.shape[1]
    local = bq_ref.shape[1] // 3
    pack_ref[0:1, :] = jnp.sum(grad * unit, axis=0, keepdims=True)
    pack_ref[1:2, :] = jnp.sum(grad, axis=0, keepdims=True)
    pack_ref[2:5, :] = s2_ref[0:3, :]
    pack_ref[5:6, :] = bd_ref[...]
    for i in range(hidden // width):
        pack_ref[6 + i : 7 + i, :] = bu_ref[:, i * width : (i + 1) * width]
    after = 6 + hidden // width
    pack_ref[after : after + 1, :local] = bq_ref[:, :local]
    pack_ref[after : after + 1, local:] = bq_ref[:, 2 * local :]
    pack_ref[after + 1 :, :] = jnp.zeros((pack_ref.shape[0] - after - 1, width), F32)


def images_back(chain, x, gain, gr, ga, gb, bd, bu, s2, bq):
    return chain(
        images_back_kernel,
        (x, gain, gr, ga, gb, bd, bu, s2, bq),
        [VM] * 9,
        (shape_of(x.shape, BF), shape_of((16, x.shape[1]), F32)),
        (VM, VM),
        name="images_back",
    )


def block_out_kernel(x_ref, pa_ref, pb_ref, ob_ref, ma_ref, mb_ref, db_ref, out_ref):
    resid = x_ref[...].astype(F32) + (pa_ref[...].astype(F32) + pb_ref[...].astype(F32)) + row_of(ob_ref)
    out_ref[...] = (resid + paired(ma_ref, mb_ref) + row_of(db_ref)).astype(BF)


def block_out(chain, x, pa, pb, out_bias, ma, mb, down_bias):
    return chain(
        block_out_kernel,
        (x, pa, pb, out_bias, ma, mb, down_bias),
        [VM] * 7,
        shape_of(x.shape, BF), VM, name="block_out"
    )


def add_split_kernel(where_ref, k0_ref, k1_ref, r0_ref, r1_ref, send_ref, keep_ref):
    keep_ref[...] = (k0_ref[...].astype(F32) + r0_ref[...].astype(F32)).astype(BF)
    send_ref[...] = (k1_ref[...].astype(F32) + r1_ref[...].astype(F32)).astype(BF)


def add_split(chain, where, bit, keep, recv):
    rows, width = keep.shape
    half = rows // 2
    block = (half, width)
    own = pl.BlockSpec(block, lambda i, w: (side_of(w, bit), 0))
    other = pl.BlockSpec(block, lambda i, w: (1 - side_of(w, bit), 0))
    out = pl.BlockSpec(block, lambda i, w: (0, 0))
    return chain(
        add_split_kernel,
        (where, keep, keep, recv, recv),
        [own, other, own, other],
        (shape_of((half, width), BF),) * 2,
        (out, out),
        grid=(1,),
        name="add_split",
        prefetch=1,
        vmem=16,
    )


def add_kernel(a_ref, b_ref, out_ref):
    out_ref[...] = (a_ref[...].astype(F32) + b_ref[...].astype(F32)).astype(out_ref.dtype)


def add(chain, a, b):
    return chain(add_kernel, (a, b), [VM, VM], shape_of(a.shape, a.dtype), VM, name="add", vmem=16)


def join(chain, where, bit, own, other):
    half, width = own.shape

    def body(where_ref, own_ref, other_ref, out_ref):
        side = side_of(where_ref, bit)
        out_ref[pl.ds(pl.multiple_of(side * half, 16), half), :] = own_ref[...]
        out_ref[pl.ds(pl.multiple_of((1 - side) * half, 16), half), :] = other_ref[...]

    return chain(
        body,
        (where, own, other),
        [VM, VM],
        shape_of((2 * half, width), BF),
        VM,
        name="join",
        prefetch=1,
        vmem=16,
    )


class Home:
    def __init__(self, shape):
        self.shape, self.now = shape, None


def finish(chain, where, bits, flip, piece, homes):
    half, width = piece.shape
    parts = 4
    block = half // parts
    targets = list(dict.fromkeys(home for home, _ in homes))
    old = [home for home in targets if home.now is not None]

    def body(where_ref, piece_ref, *rest):
        outs = rest[len(old) : len(old) + len(targets)]
        made, sems = rest[-2:]
        which = side_of(where_ref, bits) ^ flip

        def write(number):
            home, row = homes[number]
            out_ref = outs[targets.index(home)]
            copies = []
            for i in range(parts):
                made[i * block : (i + 1) * block, :] = piece_ref[i * block : (i + 1) * block, :].astype(F32)
                if home.shape[1] == width:
                    place = out_ref.at[pl.ds(row + i * block, block)]
                else:
                    high = home.shape[0]
                    place = out_ref.at[pl.ds(i * block % high, block), pl.ds(i * block // high * width, width)]
                copies.append(pltpu.make_async_copy(made.at[pl.ds(i * block, block)], place, sems.at[i]))
                copies[-1].start()
            for copy in copies:
                copy.wait()

        for number in range(2):

            @pl.when(which == number)
            def _(number=number):
                write(number)

    made = chain(
        body,
        (where, piece, *(home.now for home in old)),
        [VM] + [HBM] * len(old),
        tuple(shape_of(home.shape, F32) for home in targets) + (shape_of((8, 128), F32),),
        (HBM,) * (len(targets) + 1),
        [pltpu.VMEM((half, width), F32), pltpu.SemaphoreType.DMA((parts,))],
        aliases={2 + i: targets.index(home) for i, home in enumerate(old)},
        name="finish",
        prefetch=1,
        vmem=16,
    )
    for home, now in zip(targets, made[:-1], strict=True):
        home.now = now
    chain.last = made[-1]


def unpack(chain, pack, hidden, local):
    width = pack.shape[1]
    steps = hidden // width

    def body(pack_ref, *outs):
        for i in range(6):
            outs[i][...] = pack_ref[i, :]
        for i in range(steps):
            outs[6][i * width : (i + 1) * width] = pack_ref[6 + i, :]
        for i in range(2):
            outs[7][i : i + 1, :] = pack_ref[6 + steps : 7 + steps, i * local : (i + 1) * local]

    line = shape_of((width,), F32)
    return chain(
        body,
        (pack,),
        [VM],
        (line,) * 6 + (shape_of((hidden,), F32), shape_of((2, local), F32)),
        (VM,) * 8,
        name="unpack",
    )


class Lane:
    def __init__(self, chain, where, order, homes):
        self.chain, self.where, self.homes = chain, where, homes
        self.bits = list(zip(*order, strict=True))
        self.keep = self.send = None
        self.stage = 0

    def begin(self, keep, send):
        self.keep, self.send = keep, send

    def over(self, bits, piece):
        pairs = [
            (2 * i + core, 2 * (i ^ (1 << bits[core])) + core) for i in range(lax.axis_size("dp")) for core in range(2)
        ]
        return lax.ppermute(piece, ("dp", "tensor"), pairs)

    def step(self):
        stage, bits, chain = self.stage, self.bits, self.chain
        self.stage += 1
        if stage < 2:
            recv = self.over(bits[stage], self.send)
            self.send, self.keep = add_split(chain, self.where, bits[stage + 1], self.keep, recv)
        elif stage == 2:
            self.keep = add(chain, self.keep, self.over(bits[2], self.send))
        elif stage == 3:
            self.keep = add(chain, self.keep, self.over((3, 3), self.keep))
        elif stage < 6:
            bit = bits[6 - stage]
            self.keep = join(chain, self.where, bit, self.keep, self.over(bit, self.keep))
        elif stage == 6:
            self.send = self.over(bits[0], self.keep)
            finish(chain, self.where, bits[0], 0, self.keep, self.homes)
        else:
            finish(chain, self.where, bits[0], 1, self.send, self.homes)


ORDERS = {
    "D0": ((0, 1, 2), (1, 0, 2)),
    "D1": ((2, 0, 1), (2, 0, 1)),
    "U0": ((1, 2, 0), (0, 1, 2)),
    "U1": ((2, 1, 0), (1, 0, 2)),
    "Q0": ((1, 0, 2), (0, 1, 2)),
    "Q1": ((0, 1, 2), (2, 1, 0)),
}
SCHEDULE = (
    "down", "resid_back", "D0", "attend_back", "q_send", "D1", "q_keep", "back_in", "U0", "D0",
    "block_out", "U1", "Q1", "D0", "Q0", "images_back", "Q1", "D0", "U0", "D1", "Q1", "pack0", "D0",
    "D1", "Q1", "U1", "U0", "D1", "U1", "Q1", "Q0", "D0", "U0", "D1", "pack1", "Q0", "D0", "U1", "U0",
    "Q0", "Q1", "U1", "Q0", "D1", "D1", "U0", "D0", "Q0", "Q1", "pack2", "U1", "U0", "Q0", "U1", "D1",
    "pack3", "unpack", "Q1", "U0", "Q0", "U1",
)


def shards_cube(
    images,
    image_mask,
    cotangent,
    ln1_gain,
    ln1_bias,
    w_qkv,
    qv_bias,
    w_out,
    out_bias,
    ln2_gain,
    ln2_bias,
    w_up,
    up_bias,
    w_down,
    down_bias,
):
    _, rows, width = images.shape
    local = w_qkv.shape[2]
    hidden = w_up.shape[1]
    x = images.reshape(rows, width)
    cot = cotangent.reshape(rows, width)
    where = jnp.stack([lax.axis_index("dp"), lax.axis_index("tensor")]).astype(jnp.int32)
    w3 = jnp.transpose(w_qkv, (1, 0, 2))
    chain = Chain()

    def swapped(piece):
        return lax.ppermute(piece, "tensor", [(0, 1), (1, 0)])

    downs, ups, outs = Home((hidden, width)), Home((width, hidden)), Home((local, width))
    projections = Home((3 * width, local))
    places = {
        "D0": ((downs, 0), (downs, hidden // 4)),
        "D1": ((downs, hidden // 2), (downs, 3 * hidden // 4)),
        "U0": ((ups, 0), (ups, width // 4)),
        "U1": ((ups, width // 2), (ups, 3 * width // 4)),
        "Q0": ((projections, 0), (projections, width)),
        "Q1": ((projections, 2 * width), (outs, 0)),
    }
    lanes = {name: Lane(chain, where, ORDERS[name], homes) for name, homes in places.items()}
    first = {name: lane.bits[0] for name, lane in lanes.items()}

    part, q, k, v, mixed, n1, lse, ga, go, bd = attend(
        chain, image_mask, ln1_gain, ln1_bias, qv_bias, x, w3, w_out, cot, w_down
    )
    part_b = swapped(part)
    bits = [first[name] for name in ("D0", "D1", "U0", "U1")]
    act, gn2, ds0, ds1, dk0, dk1, us0, us1, uk0, uk1, bu = feed(
        chain, where, bits, out_bias, ln2_gain, ln2_bias, up_bias, x, part, part_b, go, w_up, ga
    )
    for name, keep, send in (("D0", dk0, ds0), ("D1", dk1, ds1), ("U0", uk0, us0), ("U1", uk1, us1)):
        lanes[name].begin(keep, send)
    gn2_b = swapped(gn2)
    qkv = (first["Q0"], first["Q1"])
    have = {}

    def compute(name):
        if name == "down":
            have["mlp"] = down(chain, act, w_down)
            have["mlpb"] = swapped(have["mlp"])
        elif name == "resid_back":
            have["gr"], have["gm"], have["s2"], have["og"] = resid_back(
                chain, x, part, part_b, out_bias, ln2_gain, gn2, gn2_b, go, mixed, w_out
            )
        elif name == "attend_back":
            have["grads"], have["bq"] = attend_back(chain, q, k, v, mixed, have["gm"], lse)
        elif name == "q_send":
            have["qs"] = qkv_grad(chain, where, n1, have["grads"], have["og"], qkv, 1)
        elif name == "q_keep":
            kept = qkv_grad(chain, where, n1, have["grads"], have["og"], qkv, 0)
            for i in range(2):
                lanes["Q%d" % i].begin(kept[i], have["qs"][i])
        elif name == "back_in":
            have["gn1"] = back_in(chain, have["grads"], w3, rows)
            have["gn1b"] = swapped(have["gn1"])
        elif name == "images_back":
            have["out"], have["pack"] = images_back(
                chain, x, ln1_gain, have["gr"], have["gn1"], have["gn1b"], bd, bu, have["s2"], have["bq"]
            )
        elif name == "block_out":
            have["block"] = block_out(chain, x, part, part_b, out_bias, have["mlp"], have["mlpb"], down_bias)
        elif name[:4] == "pack":
            have["pack"] = add(chain, have["pack"], lax.ppermute(have["pack"], "dp", xor_pairs(1 << int(name[4]))))
        elif name == "unpack":
            have["small"] = unpack(chain, have["pack"], hidden, local)

    for name in SCHEDULE:
        if name in lanes:
            lanes[name].step()
        else:
            compute(name)
    small = have["small"]
    return (
        have["block"].reshape(images.shape),
        have["out"].reshape(images.shape),
        small[0],
        small[1],
        jnp.transpose(projections.now.reshape(3, width, local), (1, 0, 2)),
        small[7],
        outs.now,
        small[2],
        small[3],
        small[4],
        ups.now,
        small[6],
        downs.now,
        small[5],
    )


def shards(*args):
    images, w_up = args[0], args[11]
    cube = lax.axis_size("dp") == 16 and lax.axis_size("tensor") == 2
    if cube and images.shape[0] == 1 and w_up.shape[1] == 2 * w_up.shape[0]:
        return shards_cube(*args)
    return shards_any(*args)


def solution(mesh):
    in_specs = (
        P("dp", None, None),
        P("dp"),
        P("dp", None, None),
        P(),
        P(),
        P(None, None, "tensor"),
        P(None, "tensor"),
        P("tensor", None),
        P(),
        P(),
        P(),
        P(None, "tensor"),
        P("tensor"),
        P("tensor", None),
        P(),
    )
    out_specs = (
        P("dp", None, None),
        P("dp", None, None),
        P(),
        P(),
        P(None, None, "tensor"),
        P(None, "tensor"),
        P("tensor", None),
        P(),
        P(),
        P(),
        P(None, "tensor"),
        P("tensor"),
        P("tensor", None),
        P(),
    )
    return jax.shard_map(shards, mesh=mesh, in_specs=in_specs, out_specs=out_specs, check_vma=False)
```

profile of v0, /device:TPU:0, one launch (start us, length us, event | category | flops | bytes accessed | tf_op | source)
XLA Modules:
  0.0 279.9 jit_solution(2785893328623222907)
XLA Ops:
  1.3 18.2 %attend.1 = (bf16[584,1024]{1,0:T(8,128)(2,1)}, bf16[592,512]{1,0:T(8,128)(2,1)}, bf16[592,512]{1,0:T(8,128)(2,1)}, bf16[592,512]{1,0:T(8,128)(2,1)}, bf16[592,5...) custom-call(s32[1]{0:T(128)S(6)} %copy.49.mask_ref, ...), custom_call_target="tpu_custom_call" | custom-call | bytes 3000 | tf_op jit(solution)/shard_map/attend/pallas_call | solution.py:308
  23.7 25.4 %feed.1 = (bf16[584,2048]{1,0:T(8,128)(2,1)}, bf16[584,1024]{1,0:T(8,128)(2,1)}, bf16[512,1024]{1,0:T(8,128)(2,1)}, bf16[512,1024]{1,0:T(8,128)(2,1)}, bf16[512,...) custom-call(s32[2]{0:T(128)} %pad_add_fusion.refs_0_, ...), custom_call_target="tpu_custom_call" | custom-call | bytes 3000 | tf_op jit(solution)/shard_map/feed/pallas_call | solution.py:308
  59.2 3.0 %down.1.refs_10_.refs_4_ = bf16[584,1024]{1,0:T(8,128)(2,1)S(1)} custom-call(bf16[584,2048]{1,0:T(8,128)(2,1)S(1)} %copy-done.6, bf16[2048,1024]{1,0:T(8,128)(2,1)S(1)} %copy-done.2, bf16[584,2048]{1,0:T(8,128)(2,1)S(1)} %copy-done.6), custom_call_target="tpu_custom_call" | custom-call | bytes 3000 | tf_op jit(solution)/shard_map/down/pallas_call | solution.py:308
  63.7 3.9 %resid_back.1 = (f32[584,1024]{1,0:T(8,128)S(1)}, bf16[592,512]{1,0:T(8,128)(2,1)S(1)}, f32[8,1024]{1,0:T(8,128)S(1)}, bf16[1024,512]{1,0:T(8,128)(2,1)S(1)}) custom-call(bf16[584,1024]{1,0:T(8,128)(2,1)S(1)} %bitcast.12, bf16[584,1024]{1,0:T(8,128)(2,1)S(1)} %copy-done.1, bf16[584,1024]{1,0:T(8,128)(2,1)S(1)} %copy-done.5, bf16[1024]{0:T(1024)(128)(2,1)S(1)} %copy-done.29, ...), custom_call_target="tpu_custom_call" | custom-call | bytes 3000 | tf_op jit(solution)/shard_map/resid_back/pallas_call | solution.py:308
  67.6 6.5 %collective-permute-done.2.refs_3_.refs_4_ = bf16[512,1024]{1,0:T(8,128)(2,1)S(1)} collective-permute-done((bf16[512,1024]{1,0:T(8,128)(2,1)}, bf16[512,1024]{1,0:T(8,128)(2,1)S(1)}, u32[]{:S(2)}, u32[]{:S(2)}) %collective-permute-start.2) | collective-permute-done | bytes 1048608 | tf_op jit(solution)/shard_map/ppermute | solution.py:947
  75.6 3.5 %collective-permute-start.4 = (bf16[256,1024]{1,0:T(8,128)(2,1)}, bf16[256,1024]{1,0:T(8,128)(2,1)}, u32[]{:S(2)}, u32[]{:S(2)}) collective-permute-start(bf16[256,1024]{1,0:T(8,128)(2,1)} %get-tuple-element.114.refs_6_), channel_id=1, source_target_pairs={{0,4},{1,3},{2,6},{3,1},{4,0},{5,7},{6,2},{7,5},{8,12},{9,11},{10,... | collective-permute-start | bytes 1572872 | tf_op jit(solution)/shard_map/ppermute | solution.py:947
  81.2 9.3 %attend_back.1 = (bf16[592,1536]{1,0:T(8,128)(2,1)S(1)}, f32[1,1536]{1,0:T(1,128)S(1)}) custom-call(bf16[592,512]{1,0:T(8,128)(2,1)S(1)} %copy-done.23, bf16[592,512]{1,0:T(8,128)(2,1)S(1)} %copy-done.24, bf16[592,512]{1,0:T(8,128)(2,1)S(1)} %copy-done.25, bf16[592,512]{1,0:T(8,128)(2,1)S(1)} %copy-done.19, bf16[592,512]{1,0:T(8,128)(2,1)S(1)} %get-tuple-element.120.refs_4_, ...), custom_call_target="tpu_custom_call" | custom-call | bytes 3000 | tf_op jit(solution)/shard_map/attend_back/pallas_call | solution.py:308
  100.9 5.0 %back_in.1.refs_5_.refs_3_ = bf16[584,1024]{1,0:T(8,128)(2,1)S(1)} custom-call(bf16[592,1536]{1,0:T(8,128)(2,1)S(1)} %get-tuple-element.122.refs_2_.refs_4_.refs_0_, bf16[3,1024,512]{2,1,0:T(8,128)(2,1)S(1)} %bitcast.16, bf16[1024,512]{1,0:T(8,128)(2,1)S(1)} %get-tuple-element.129.refs_2_.refs_1_), custom_call_target="tpu_custom_call" | custom-call | bytes 3000 | tf_op jit(solution)/shard_map/back_in/pallas_call | solution.py:308
  108.7 3.3 %block_out.1.refs_5_ = bf16[584,1024]{1,0:T(8,128)(2,1)} custom-call(bf16[584,1024]{1,0:T(8,128)(2,1)S(1)} %bitcast.13, bf16[584,1024]{1,0:T(8,128)(2,1)S(1)} %copy-done.1, bf16[584,1024]{1,0:T(8,128)(2,1)S(1)} %copy-done.5, bf16[1024]{0:T(1024)(128)(2,1)S(1)} %copy-done.29, bf16[584,1024]{1,0:T(8,128)(2,1)S(1)} %down.1.refs_10_.refs_4_, ...), custom_call_target="tpu_custom_call" | custom-call | bytes 3000 | tf_op jit(solution)/shard_map/block_out/pallas_call | solution.py:308
  115.3 4.3 %collective-permute-done.10.refs_3_.refs_4_ = bf16[1024,512]{1,0:T(8,128)(2,1)S(1)} collective-permute-done((bf16[1024,512]{1,0:T(8,128)(2,1)}, bf16[1024,512]{1,0:T(8,128)(2,1)S(1)}, u32[]{:S(2)}, u32[]{:S(2)}) %collective-permute-start.10) | collective-permute-done | bytes 1048608 | tf_op jit(solution)/shard_map/ppermute | solution.py:947
  125.2 3.1 %images_back.1 = (bf16[584,1024]{1,0:T(8,128)(2,1)}, f32[16,1024]{1,0:T(8,128)S(1)}) custom-call(bf16[584,1024]{1,0:T(8,128)(2,1)S(1)} %bitcast.14, bf16[1024]{0:T(1024)(128)(2,1)S(1)} %copy-done.32, f32[584,1024]{1,0:T(8,128)S(1)} %get-tuple-element.112.refs_5_.refs_2_, bf16[584,1024]{1,0:T(8,128)(2,1)S(1)} %back_in.1.refs_5_.refs_3_, ...), custom_call_target="tpu_custom_call" | custom-call | bytes 3000 | tf_op jit(solution)/shard_map/images_back/pallas_call | solution.py:308
  128.3 7.0 %collective-permute-done.13.refs_3_.refs_4_ = bf16[512,512]{1,0:T(8,128)(2,1)S(1)} collective-permute-done((bf16[512,512]{1,0:T(8,128)(2,1)S(1)}, bf16[512,512]{1,0:T(8,128)(2,1)S(1)}, u32[]{:S(2)}, u32[]{:S(2)}) %collective-permute-start.13) | collective-permute-done | bytes 524320 | tf_op jit(solution)/shard_map/ppermute | solution.py:947
  148.4 7.5 %collective-permute-done.20.refs_2_ = bf16[128,1024]{1,0:T(8,128)(2,1)S(1)} collective-permute-done((bf16[128,1024]{1,0:T(8,128)(2,1)S(1)}, bf16[128,1024]{1,0:T(8,128)(2,1)S(1)}, u32[]{:S(2)}, u32[]{:S(2)}) %collective-permute-start.20) | collective-permute-done | bytes 262176 | tf_op jit(solution)/shard_map/ppermute | solution.py:947
  156.7 4.4 %collective-permute-done.24.refs_1_ = bf16[256,512]{1,0:T(8,128)(2,1)S(1)} collective-permute-done((bf16[256,512]{1,0:T(8,128)(2,1)S(1)}, bf16[256,512]{1,0:T(8,128)(2,1)S(1)}, u32[]{:S(2)}, u32[]{:S(2)}) %collective-permute-start.24) | collective-permute-done | bytes 262176 | tf_op jit(solution)/shard_map/ppermute | solution.py:947
  163.7 11.3 %collective-permute-done.21.refs_1_ = bf16[128,1024]{1,0:T(8,128)(2,1)S(1)} collective-permute-done((bf16[128,1024]{1,0:T(8,128)(2,1)S(1)}, bf16[128,1024]{1,0:T(8,128)(2,1)S(1)}, u32[]{:S(2)}, u32[]{:S(2)}) %collective-permute-start.21) | collective-permute-done | bytes 262176 | tf_op jit(solution)/shard_map/ppermute | solution.py:947
  176.5 3.4 %collective-permute-start.33 = (bf16[256,512]{1,0:T(8,128)(2,1)S(1)}, bf16[256,512]{1,0:T(8,128)(2,1)S(1)}, u32[]{:S(2)}, u32[]{:S(2)}) collective-permute-start(bf16[256,512]{1,0:T(8,128)(2,1)S(1)} %get-tuple-element.159.refs_3_), channel_id=1, source_target_pairs={{0,8},{1,9},{2,10},{3,11},{4,12},{5,13},{6,14},{7,15},{8,0},{9,1},... | collective-permute-start | bytes 786440 | tf_op jit(solution)/shard_map/ppermute | solution.py:947
  182.6 8.1 %collective-permute-done.26.refs_1_ = bf16[64,2048]{1,0:T(8,128)(2,1)S(1)} collective-permute-done((bf16[64,2048]{1,0:T(8,128)(2,1)S(1)}, bf16[64,2048]{1,0:T(8,128)(2,1)S(1)}, u32[]{:S(2)}, u32[]{:S(2)}) %collective-permute-start.26) | collective-permute-done | bytes 262176 | tf_op jit(solution)/shard_map/ppermute | solution.py:947
  193.6 3.0 %collective-permute-start.34 = (bf16[256,512]{1,0:T(8,128)(2,1)S(1)}, bf16[256,512]{1,0:T(8,128)(2,1)S(1)}, u32[]{:S(2)}, u32[]{:S(2)}) collective-permute-start(bf16[256,512]{1,0:T(8,128)(2,1)S(1)} %add.29.refs_2_.refs_0_), channel_id=1, source_target_pairs={{0,16},{1,17},{2,18},{3,19},{4,20},{5,21},{6,22},{7,23},{8,24},{9,... | collective-permute-start | bytes 786440 | tf_op jit(solution)/shard_map/ppermute | solution.py:947
  198.5 5.4 %collective-permute-done.36.refs_1_ = bf16[64,2048]{1,0:T(8,128)(2,1)S(1)} collective-permute-done((bf16[64,2048]{1,0:T(8,128)(2,1)S(1)}, bf16[64,2048]{1,0:T(8,128)(2,1)S(1)}, u32[]{:S(2)}, u32[]{:S(2)}) %collective-permute-start.36) | collective-permute-done | bytes 262176 | tf_op jit(solution)/shard_map/ppermute | solution.py:947
  209.6 8.2 %collective-permute-done.38.refs_2_ = bf16[64,2048]{1,0:T(8,128)(2,1)S(1)} collective-permute-done((bf16[64,2048]{1,0:T(8,128)(2,1)S(1)}, bf16[64,2048]{1,0:T(8,128)(2,1)S(1)}, u32[]{:S(2)}, u32[]{:S(2)}) %collective-permute-start.38) | collective-permute-done | bytes 262176 | tf_op jit(solution)/shard_map/ppermute | solution.py:947
  220.9 8.1 %collective-permute-done.41.refs_2_ = bf16[256,1024]{1,0:T(8,128)(2,1)S(1)} collective-permute-done((bf16[256,1024]{1,0:T(8,128)(2,1)S(1)}, bf16[256,1024]{1,0:T(8,128)(2,1)S(1)}, u32[]{:S(2)}, u32[]{:S(2)}) %collective-permute-start.41) | collective-permute-done | bytes 524320 | tf_op jit(solution)/shard_map/ppermute | solution.py:947
  236.5 3.7 %collective-permute-done.39.refs_2_ = bf16[512,512]{1,0:T(8,128)(2,1)S(1)} collective-permute-done((bf16[512,512]{1,0:T(8,128)(2,1)S(1)}, bf16[512,512]{1,0:T(8,128)(2,1)S(1)}, u32[]{:S(2)}, u32[]{:S(2)}) %collective-permute-start.39) | collective-permute-done | bytes 524320 | tf_op jit(solution)/shard_map/ppermute | solution.py:947
  243.5 11.6 %collective-permute-done.31.refs_1_ = f32[16,1024]{1,0:T(8,128)S(1)} collective-permute-done((f32[16,1024]{1,0:T(8,128)S(1)}, f32[16,1024]{1,0:T(8,128)S(1)}, u32[]{:S(2)}, u32[]{:S(2)}) %collective-permute-start.31) | collective-permute-done | bytes 65568 | tf_op jit(solution)/shard_map/ppermute | solution.py:1068
  266.4 4.1 %collective-permute-done.43.refs_1_ = f32[16,1024]{1,0:T(8,128)S(1)} collective-permute-done((f32[16,1024]{1,0:T(8,128)S(1)}, f32[16,1024]{1,0:T(8,128)S(1)}, u32[]{:S(2)}, u32[]{:S(2)}) %collective-permute-start.43) | collective-permute-done | bytes 65568 | tf_op jit(solution)/shard_map/ppermute | solution.py:1068
  (212 shorter events, 106.1 us)
Async XLA Ops:
  49.6 24.5 %collective-permute-start.2 = (bf16[512,1024]{1,0:T(8,128)(2,1)}, bf16[512,1024]{1,0:T(8,128)(2,1)S(1)}, u32[]{:S(2)}, u32[]{:S(2)}) collective-permute-start(bf16[512,1024]{1,0:T(8,128)(2,1)} %get-tuple-element.109), channel_id=1, source_target_pairs={{0,2},{1,5},{2,0},{3,7},{4,6},{5,1},{6,4},{7,3},{8,10},{9,13},{10,... | collective-permute-start | bytes 3145736 | tf_op jit(solution)/shard_map/ppermute | solution.py:947
  52.2 41.4 %collective-permute-start.6 = (bf16[512,1024]{1,0:T(8,128)(2,1)}, bf16[512,1024]{1,0:T(8,128)(2,1)S(1)}, u32[]{:S(2)}, u32[]{:S(2)}) collective-permute-start(bf16[512,1024]{1,0:T(8,128)(2,1)} %get-tuple-element.126), channel_id=1, source_target_pairs={{0,8},{1,9},{2,10},{3,11},{4,12},{5,13},{6,14},{7,15},{8,0},{9,1},... | collective-permute-start | bytes 3145736 | tf_op jit(solution)/shard_map/ppermute | solution.py:947
  53.7 42.4 %collective-permute-start.5 = (bf16[256,2048]{1,0:T(8,128)(2,1)}, bf16[256,2048]{1,0:T(8,128)(2,1)S(1)}, u32[]{:S(2)}, u32[]{:S(2)}) collective-permute-start(bf16[256,2048]{1,0:T(8,128)(2,1)} %get-tuple-element.116), channel_id=1, source_target_pairs={{0,4},{1,3},{2,6},{3,1},{4,0},{5,7},{6,2},{7,5},{8,12},{9,11},{10,... | collective-permute-start | bytes 3145736 | tf_op jit(solution)/shard_map/ppermute | solution.py:947
  62.2 46.4 %collective-permute-start.1 = (bf16[584,1024]{1,0:T(8,128)(2,1)S(1)}, bf16[584,1024]{1,0:T(8,128)(2,1)}, u32[]{:S(2)}, u32[]{:S(2)}) collective-permute-start(bf16[584,1024]{1,0:T(8,128)(2,1)S(1)} %down.1.refs_10_.refs_4_), channel_id=1, source_target_pairs={{0,1},{1,0},{2,3},{3,2},{4,5},{5,4},{6,7},{7,6},{8,9},{9,8},{10,11... | collective-permute-start | bytes 3588104 | tf_op jit(solution)/shard_map/ppermute | solution.py:1013
  75.6 30.4 %collective-permute-start.4 = (bf16[256,1024]{1,0:T(8,128)(2,1)}, bf16[256,1024]{1,0:T(8,128)(2,1)}, u32[]{:S(2)}, u32[]{:S(2)}) collective-permute-start(bf16[256,1024]{1,0:T(8,128)(2,1)} %get-tuple-element.114.refs_6_), channel_id=1, source_target_pairs={{0,4},{1,3},{2,6},{3,1},{4,0},{5,7},{6,2},{7,5},{8,12},{9,11},{10,... | collective-permute-start | bytes 1572872 | tf_op jit(solution)/shard_map/ppermute | solution.py:947
  79.1 32.9 %collective-permute-start.11 = (bf16[256,2048]{1,0:T(8,128)(2,1)}, bf16[256,2048]{1,0:T(8,128)(2,1)}, u32[]{:S(2)}, u32[]{:S(2)}) collective-permute-start(bf16[256,2048]{1,0:T(8,128)(2,1)} %get-tuple-element.140), channel_id=1, source_target_pairs={{0,8},{1,5},{2,10},{3,7},{4,12},{5,1},{6,14},{7,3},{8,0},{9,13},{1... | collective-permute-start | bytes 3145736 | tf_op jit(solution)/shard_map/ppermute | solution.py:947
  93.5 26.0 %collective-permute-start.10 = (bf16[1024,512]{1,0:T(8,128)(2,1)}, bf16[1024,512]{1,0:T(8,128)(2,1)S(1)}, u32[]{:S(2)}, u32[]{:S(2)}) collective-permute-start(bf16[1024,512]{1,0:T(8,128)(2,1)} %get-tuple-element.138), channel_id=1, source_target_pairs={{0,2},{1,9},{2,0},{3,11},{4,6},{5,13},{6,4},{7,15},{8,10},{9,1},{1... | collective-permute-start | bytes 3145736 | tf_op jit(solution)/shard_map/ppermute | solution.py:947
  97.1 25.1 %collective-permute-start.8 = (bf16[1024,512]{1,0:T(8,128)(2,1)}, bf16[1024,512]{1,0:T(8,128)(2,1)S(1)}, u32[]{:S(2)}, u32[]{:S(2)}) collective-permute-start(bf16[1024,512]{1,0:T(8,128)(2,1)} %get-tuple-element.127.refs_5_), channel_id=1, source_target_pairs={{0,4},{1,3},{2,6},{3,1},{4,0},{5,7},{6,2},{7,5},{8,12},{9,11},{10,... | collective-permute-start | bytes 3145736 | tf_op jit(solution)/shard_map/ppermute | solution.py:947
  120.9 20.6 %collective-permute-start.15 = (bf16[256,1024]{1,0:T(8,128)(2,1)S(1)}, bf16[256,1024]{1,0:T(8,128)(2,1)S(1)}, u32[]{:S(2)}, u32[]{:S(2)}) collective-permute-start(bf16[256,1024]{1,0:T(8,128)(2,1)S(1)} %copy-done.27), channel_id=1, source_target_pairs={{0,2},{1,3},{2,0},{3,1},{4,6},{5,7},{6,4},{7,5},{8,10},{9,11},{10,... | collective-permute-start | bytes 1572872 | tf_op jit(solution)/shard_map/ppermute | solution.py:947
  137.6 23.5 %collective-permute-start.23 = (bf16[128,2048]{1,0:T(8,128)(2,1)S(1)}, bf16[128,2048]{1,0:T(8,128)(2,1)S(1)}, u32[]{:S(2)}, u32[]{:S(2)}) collective-permute-start(bf16[128,2048]{1,0:T(8,128)(2,1)S(1)} %get-tuple-element.141.refs_5_), channel_id=1, source_target_pairs={{0,4},{1,3},{2,6},{3,1},{4,0},{5,7},{6,2},{7,5},{8,12},{9,11},{10,... | collective-permute-start | bytes 1572872 | tf_op jit(solution)/shard_map/ppermute | solution.py:947
  155.9 19.9 %collective-permute-start.28 = (bf16[512,512]{1,0:T(8,128)(2,1)S(1)}, bf16[512,512]{1,0:T(8,128)(2,1)S(1)}, u32[]{:S(2)}, u32[]{:S(2)}) collective-permute-start(bf16[512,512]{1,0:T(8,128)(2,1)S(1)} %get-tuple-element.143.refs_9_), channel_id=1, source_target_pairs={{0,2},{1,5},{2,0},{3,7},{4,6},{5,1},{6,4},{7,3},{8,10},{9,13},{10,... | collective-permute-start | bytes 1572872 | tf_op jit(solution)/shard_map/ppermute | solution.py:947
  156.5 25.4 %collective-permute-start.27 = (bf16[256,1024]{1,0:T(8,128)(2,1)S(1)}, bf16[256,1024]{1,0:T(8,128)(2,1)S(1)}, u32[]{:S(2)}, u32[]{:S(2)}) collective-permute-start(bf16[256,1024]{1,0:T(8,128)(2,1)S(1)} %join.12.refs_2_.refs_1_), channel_id=1, source_target_pairs={{0,4},{1,3},{2,6},{3,1},{4,0},{5,7},{6,2},{7,5},{8,12},{9,11},{10,... | collective-permute-start | bytes 1572872 | tf_op jit(solution)/shard_map/ppermute | solution.py:947
  181.9 25.1 %collective-permute-start.32 = (bf16[512,512]{1,0:T(8,128)(2,1)S(1)}, bf16[512,512]{1,0:T(8,128)(2,1)S(1)}, u32[]{:S(2)}, u32[]{:S(2)}) collective-permute-start(bf16[512,512]{1,0:T(8,128)(2,1)S(1)} %join.13.refs_5_.refs_1_), channel_id=1, source_target_pairs={{0,4},{1,5},{2,6},{3,7},{4,0},{5,1},{6,2},{7,3},{8,12},{9,13},{10,... | collective-permute-start | bytes 1572872 | tf_op jit(solution)/shard_map/ppermute | solution.py:947
  191.4 43.1 %collective-permute-start.40 = (bf16[512,1024]{1,0:T(8,128)(2,1)S(1)}, bf16[512,1024]{1,0:T(8,128)(2,1)S(1)}, u32[]{:S(2)}, u32[]{:S(2)}) collective-permute-start(bf16[512,1024]{1,0:T(8,128)(2,1)S(1)} %join.14.refs_2_.refs_1_), channel_id=1, source_target_pairs={{0,2},{1,5},{2,0},{3,7},{4,6},{5,1},{6,4},{7,3},{8,10},{9,13},{10,... | collective-permute-start | bytes 3145736 | tf_op jit(solution)/shard_map/ppermute | solution.py:947
  206.9 22.1 %collective-permute-start.41 = (bf16[256,1024]{1,0:T(8,128)(2,1)S(1)}, bf16[256,1024]{1,0:T(8,128)(2,1)S(1)}, u32[]{:S(2)}, u32[]{:S(2)}) collective-permute-start(bf16[256,1024]{1,0:T(8,128)(2,1)S(1)} %join.15.refs_2_.refs_1_), channel_id=1, source_target_pairs={{0,2},{1,3},{2,0},{3,1},{4,6},{5,7},{6,4},{7,5},{8,10},{9,11},{10,... | collective-permute-start | bytes 1572872 | tf_op jit(solution)/shard_map/ppermute | solution.py:947
  207.0 24.3 %collective-permute-start.42 = (bf16[128,2048]{1,0:T(8,128)(2,1)S(1)}, bf16[128,2048]{1,0:T(8,128)(2,1)S(1)}, u32[]{:S(2)}, u32[]{:S(2)}) collective-permute-start(bf16[128,2048]{1,0:T(8,128)(2,1)S(1)} %join.16.refs_2_.refs_1_), channel_id=1, source_target_pairs={{0,8},{1,5},{2,10},{3,7},{4,12},{5,1},{6,14},{7,3},{8,0},{9,13},{1... | collective-permute-start | bytes 1572872 | tf_op jit(solution)/shard_map/ppermute | solution.py:947
  218.9 21.3 %collective-permute-start.39 = (bf16[512,512]{1,0:T(8,128)(2,1)S(1)}, bf16[512,512]{1,0:T(8,128)(2,1)S(1)}, u32[]{:S(2)}, u32[]{:S(2)}) collective-permute-start(bf16[512,512]{1,0:T(8,128)(2,1)S(1)} %join.19.refs_3_.refs_1_), channel_id=1, source_target_pairs={{0,2},{1,5},{2,0},{3,7},{4,6},{5,1},{6,4},{7,3},{8,10},{9,13},{10,... | collective-permute-start | bytes 1572872 | tf_op jit(solution)/shard_map/ppermute | solution.py:947
  219.0 36.1 %collective-permute-start.45 = (bf16[128,2048]{1,0:T(8,128)(2,1)S(1)}, bf16[128,2048]{1,0:T(8,128)(2,1)S(1)}, u32[]{:S(2)}, u32[]{:S(2)}) collective-permute-start(bf16[128,2048]{1,0:T(8,128)(2,1)S(1)} %join.18.refs_3_.refs_1_), channel_id=1, source_target_pairs={{0,4},{1,3},{2,6},{3,1},{4,0},{5,7},{6,2},{7,5},{8,12},{9,11},{10,... | collective-permute-start | bytes 1572872 | tf_op jit(solution)/shard_map/ppermute | solution.py:947
  229.6 27.8 %collective-permute-start.44 = (bf16[512,1024]{1,0:T(8,128)(2,1)S(1)}, bf16[512,1024]{1,0:T(8,128)(2,1)S(1)}, u32[]{:S(2)}, u32[]{:S(2)}) collective-permute-start(bf16[512,1024]{1,0:T(8,128)(2,1)S(1)} %join.20.refs_1_.refs_3_), channel_id=1, source_target_pairs={{0,8},{1,9},{2,10},{3,11},{4,12},{5,13},{6,14},{7,15},{8,0},{9,1},... | collective-permute-start | bytes 3145736 | tf_op jit(solution)/shard_map/ppermute | solution.py:947
  231.3 23.8 %collective-permute-start.31 = (f32[16,1024]{1,0:T(8,128)S(1)}, f32[16,1024]{1,0:T(8,128)S(1)}, u32[]{:S(2)}, u32[]{:S(2)}) collective-permute-start(f32[16,1024]{1,0:T(8,128)S(1)} %add.28.refs_2_.refs_0_), channel_id=1, source_target_pairs={{0,8},{2,10},{4,12},{6,14},{8,0},{10,2},{12,4},{14,6},{16,24},{18,... | collective-permute-start | bytes 196616 | tf_op jit(solution)/shard_map/ppermute | solution.py:1068
  234.5 36.7 %collective-permute-start.47 = (bf16[1024,512]{1,0:T(8,128)(2,1)S(1)}, bf16[1024,512]{1,0:T(8,128)(2,1)S(1)}, u32[]{:S(2)}, u32[]{:S(2)}) collective-permute-start(bf16[1024,512]{1,0:T(8,128)(2,1)S(1)} %join.17.refs_3_.refs_1_), channel_id=1, source_target_pairs={{0,2},{1,9},{2,0},{3,11},{4,6},{5,13},{6,4},{7,15},{8,10},{9,1},{1... | collective-permute-start | bytes 3145736 | tf_op jit(solution)/shard_map/ppermute | solution.py:947
  240.2 33.5 %collective-permute-start.48 = (bf16[256,2048]{1,0:T(8,128)(2,1)S(1)}, bf16[256,2048]{1,0:T(8,128)(2,1)S(1)}, u32[]{:S(2)}, u32[]{:S(2)}) collective-permute-start(bf16[256,2048]{1,0:T(8,128)(2,1)S(1)} %join.21.refs_3_.refs_1_), channel_id=1, source_target_pairs={{0,4},{1,3},{2,6},{3,1},{4,0},{5,7},{6,2},{7,5},{8,12},{9,11},{10,... | collective-permute-start | bytes 3145736 | tf_op jit(solution)/shard_map/ppermute | solution.py:947
  255.1 20.6 %collective-permute-start.46 = (bf16[1024,512]{1,0:T(8,128)(2,1)S(1)}, bf16[1024,512]{1,0:T(8,128)(2,1)S(1)}, u32[]{:S(2)}, u32[]{:S(2)}) collective-permute-start(bf16[1024,512]{1,0:T(8,128)(2,1)S(1)} %join.22.refs_2_.refs_1_), channel_id=1, source_target_pairs={{0,4},{1,3},{2,6},{3,1},{4,0},{5,7},{6,2},{7,5},{8,12},{9,11},{10,... | collective-permute-start | bytes 3145736 | tf_op jit(solution)/shard_map/ppermute | solution.py:947
  255.7 21.9 %collective-permute-start.49 = (bf16[256,2048]{1,0:T(8,128)(2,1)S(1)}, bf16[256,2048]{1,0:T(8,128)(2,1)S(1)}, u32[]{:S(2)}, u32[]{:S(2)}) collective-permute-start(bf16[256,2048]{1,0:T(8,128)(2,1)S(1)} %join.23.refs_2_.refs_1_), channel_id=1, source_target_pairs={{0,8},{1,5},{2,10},{3,7},{4,12},{5,1},{6,14},{7,3},{8,0},{9,13},{1... | collective-permute-start | bytes 3145736 | tf_op jit(solution)/shard_map/ppermute | solution.py:947
  (62 other events, 526.3 us)
where the time goes:
time: 285 us; the launch traced here: 280 us
  Pallas kernels  120 us (42%)
  waiting for transfers between devices  97.3 us (34%)
  starting transfers between devices  48.2 us (17%)
  local copies, waits for them, and re-layouts  10.9 us (4%)
    pallas_call x63, Pallas kernels, __call__(): pl.pallas_call(run, out_shape=outs, grid_spec=spec, input_output_aliases=...  120 us
    ppermute x42, waiting for transfers between devices, over(): return lax.ppermute(piece, ('dp', 'tensor'), pairs)  79.5 us
    ppermute x42, starting transfers between devices, over(): return lax.ppermute(piece, ('dp', 'tensor'), pairs)  42.5 us
    ppermute x4, waiting for transfers between devices, compute(): lax.ppermute(have['pack'], 'dp', xor_pairs(1 << int(name[4])))  15.7 us
    unnamed x72, local copies, waits for them, and re-layouts  10.9 us
  transfers between devices with their start and end apart: 50, of which 16 were waited for; matrix products, arithmetic and copies ran while one was open for 0% of the time, Pallas kernels for 27%

commit v1 on v0

--- a/solution.py
+++ b/solution.py
@@ -968,18 +968,18 @@
 
 ORDERS = {
     "D0": ((0, 1, 2), (1, 0, 2)),
-    "D1": ((2, 0, 1), (2, 0, 1)),
-    "U0": ((1, 2, 0), (0, 1, 2)),
-    "U1": ((2, 1, 0), (1, 0, 2)),
-    "Q0": ((1, 0, 2), (0, 1, 2)),
-    "Q1": ((0, 1, 2), (2, 1, 0)),
+    "D1": ((0, 1, 2), (2, 0, 1)),
+    "U0": ((2, 1, 0), (1, 0, 2)),
+    "U1": ((1, 0, 2), (2, 1, 0)),
+    "Q0": ((0, 1, 2), (0, 1, 2)),
+    "Q1": ((1, 0, 2), (2, 1, 0)),
 }
 SCHEDULE = (
-    "down", "resid_back", "D0", "attend_back", "q_send", "D1", "q_keep", "back_in", "U0", "D0",
-    "block_out", "U1", "Q1", "D0", "Q0", "images_back", "Q1", "D0", "U0", "D1", "Q1", "pack0", "D0",
-    "D1", "Q1", "U1", "U0", "D1", "U1", "Q1", "Q0", "D0", "U0", "D1", "pack1", "Q0", "D0", "U1", "U0",
-    "Q0", "Q1", "U1", "Q0", "D1", "D1", "U0", "D0", "Q0", "Q1", "pack2", "U1", "U0", "Q0", "U1", "D1",
-    "pack3", "unpack", "Q1", "U0", "Q0", "U1",
+    "down", "resid_back", "U0", "attend_back", "q_send", "D0", "U0", "back_in", "D0", "D1", "U1", "D0",
+    "U0", "q_keep", "Q1", "D0", "Q0", "U0", "U1", "images_back", "Q0", "D1", "U0", "U1", "Q1", "pack0",
+    "Q0", "U1", "D1", "D0", "pack1", "Q0", "U0", "Q1", "U1", "U0", "D0", "Q1", "U1", "pack2", "D1",
+    "Q0", "block_out", "D1", "pack3", "Q1", "Q0", "D0", "D0", "Q0", "Q1", "U1", "D1", "D1", "U1", "U0",
+    "Q0", "unpack", "Q1", "D1", "Q1",
 )
 
 

time: 285 us -> 280 us (0.982)
  waiting for transfers between devices: 97.3 us -> 82 us
  starting transfers between devices: 48.2 us -> 61.7 us
  Pallas kernels: 120 us -> 117 us
    ppermute x42, starting transfers between devices: 42.5 us -> 56.6 us  [over(): return lax.ppermute(piece, ('dp', 'tensor'), pairs)]
    ppermute x4, waiting for transfers between devices: 15.7 us -> 5.38 us  [compute(): lax.ppermute(have['pack'], 'dp', xor_pairs(1 << int(name[4])))]
    ppermute x42, waiting for transfers between devices: 79.5 us -> 74.5 us  [over(): return lax.ppermute(piece, ('dp', 'tensor'), pairs)]
    pallas_call x63, Pallas kernels: 120 us -> 117 us  [__call__(): pl.pallas_call(run, out_shape=outs, grid_spec=spec, input_output_aliases=...]
    unnamed x72 -> x64, local copies, waits for them, and re-layouts: 10.9 us -> 11.8 us
  transfers between devices with their start and end apart: 50 -> 50, of which waited for: 16 -> 21; matrix products, arithmetic and copies ran while one was open for 0% -> 0% of each run, Pallas kernels for 27% -> 26%
where the time goes in v1:
time: 280 us; the launch traced here: 275 us
  Pallas kernels  117 us (42%)
  waiting for transfers between devices  82 us (29%)
  starting transfers between devices  61.7 us (22%)
  local copies, waits for them, and re-layouts  11.8 us (4%)
    pallas_call x63, Pallas kernels, __call__(): pl.pallas_call(run, out_shape=outs, grid_spec=spec, input_output_aliases=...  117 us
    ppermute x42, waiting for transfers between devices, over(): return lax.ppermute(piece, ('dp', 'tensor'), pairs)  74.5 us
    ppermute x42, starting transfers between devices, over(): return lax.ppermute(piece, ('dp', 'tensor'), pairs)  56.6 us
    unnamed x64, local copies, waits for them, and re-layouts  11.8 us
  transfers between devices with their start and end apart: 50, of which 21 were waited for; matrix products, arithmetic and copies ran while one was open for 0% of the time, Pallas kernels for 26%

profile of v1, /device:TPU:0, one launch (start us, length us, event | category | flops | bytes accessed | tf_op | source)
XLA Modules:
  0.0 275.4 jit_solution(9339567075835280375)
XLA Ops:
  1.3 18.5 %attend.1 = (bf16[584,1024]{1,0:T(8,128)(2,1)}, bf16[592,512]{1,0:T(8,128)(2,1)}, bf16[592,512]{1,0:T(8,128)(2,1)}, bf16[592,512]{1,0:T(8,128)(2,1)}, bf16[592,5...) custom-call(s32[1]{0:T(128)S(6)} %copy.49.mask_ref, ...), custom_call_target="tpu_custom_call" | custom-call | bytes 3000 | tf_op jit(solution)/shard_map/attend/pallas_call | solution.py:308
  24.0 25.0 %feed.1 = (bf16[584,2048]{1,0:T(8,128)(2,1)}, bf16[584,1024]{1,0:T(8,128)(2,1)}, bf16[512,1024]{1,0:T(8,128)(2,1)}, bf16[512,1024]{1,0:T(8,128)(2,1)}, bf16[512,...) custom-call(s32[2]{0:T(128)} %pad_add_fusion.refs_0_, ...), custom_call_target="tpu_custom_call" | custom-call | bytes 3000 | tf_op jit(solution)/shard_map/feed/pallas_call | solution.py:308
  57.7 3.0 %down.1.refs_10_.refs_4_ = bf16[584,1024]{1,0:T(8,128)(2,1)S(1)} custom-call(bf16[584,2048]{1,0:T(8,128)(2,1)S(1)} %copy-done.6, bf16[2048,1024]{1,0:T(8,128)(2,1)S(1)} %copy-done.2, bf16[584,2048]{1,0:T(8,128)(2,1)S(1)} %copy-done.6), custom_call_target="tpu_custom_call" | custom-call | bytes 3000 | tf_op jit(solution)/shard_map/down/pallas_call | solution.py:308
  64.9 3.8 %resid_back.1 = (f32[584,1024]{1,0:T(8,128)S(1)}, bf16[592,512]{1,0:T(8,128)(2,1)S(1)}, f32[8,1024]{1,0:T(8,128)S(1)}, bf16[1024,512]{1,0:T(8,128)(2,1)S(1)}) custom-call(bf16[584,1024]{1,0:T(8,128)(2,1)S(1)} %bitcast.12, bf16[584,1024]{1,0:T(8,128)(2,1)S(1)} %copy-done.1, bf16[584,1024]{1,0:T(8,128)(2,1)S(1)} %copy-done.5, bf16[1024]{0:T(1024)(128)(2,1)S(1)} %copy-done.25, ...), custom_call_target="tpu_custom_call" | custom-call | bytes 3000 | tf_op jit(solution)/shard_map/resid_back/pallas_call | solution.py:308
  72.3 9.3 %attend_back.1 = (bf16[592,1536]{1,0:T(8,128)(2,1)S(1)}, f32[1,1536]{1,0:T(1,128)S(1)}) custom-call(bf16[592,512]{1,0:T(8,128)(2,1)S(1)} %copy-done.21, bf16[592,512]{1,0:T(8,128)(2,1)S(1)} %copy-done.22, bf16[592,512]{1,0:T(8,128)(2,1)S(1)} %copy-done.23, bf16[592,512]{1,0:T(8,128)(2,1)S(1)} %copy-done.15, bf16[592,512]{1,0:T(8,128)(2,1)S(1)} %get-tuple-element.114.refs_4_, ...), custom_call_target="tpu_custom_call" | custom-call | bytes 3000 | tf_op jit(solution)/shard_map/attend_back/pallas_call | solution.py:308
  81.7 2.9 %qkv_grad.2 = (bf16[1024,512]{1,0:T(8,128)(2,1)}, bf16[1024,512]{1,0:T(8,128)(2,1)}) custom-call(s32[2]{0:T(128)S(1)} %copy-done.20, bf16[592,1024]{1,0:T(8,128)(2,1)S(1)} %copy-done.7, bf16[592,1536]{1,0:T(8,128)(2,1)S(1)} %get-tuple-element.120.refs_2_.refs_4_.refs_0_, bf16[1024,512]{1,0:T(8,128)(2,1)S(1)} %get-tuple-element.121.refs_3_, ...), custom_call_target="tpu_custom_call" | custom-call | bytes 3000 | tf_op jit(solution)/shard_map/qkv_grad/pallas_call | solution.py:308
  90.4 5.0 %back_in.1.refs_5_.refs_3_ = bf16[584,1024]{1,0:T(8,128)(2,1)S(1)} custom-call(bf16[592,1536]{1,0:T(8,128)(2,1)S(1)} %get-tuple-element.120.refs_2_.refs_4_.refs_0_, bf16[3,1024,512]{2,1,0:T(8,128)(2,1)S(1)} %bitcast.16, bf16[64,2048]{1,0:T(8,128)(2,1)S(1)} %get-tuple-element.128.refs_2_), custom_call_target="tpu_custom_call" | custom-call | bytes 3000 | tf_op jit(solution)/shard_map/back_in/pallas_call | solution.py:308
  95.4 3.2 %collective-permute-done.7.refs_3_.refs_4_ = bf16[256,1024]{1,0:T(8,128)(2,1)S(1)} collective-permute-done((bf16[256,1024]{1,0:T(8,128)(2,1)S(1)}, bf16[256,1024]{1,0:T(8,128)(2,1)S(1)}, u32[]{:S(2)}, u32[]{:S(2)}) %collective-permute-start.7) | collective-permute-done | bytes 524320 | tf_op jit(solution)/shard_map/ppermute | solution.py:947
  104.2 4.2 %collective-permute-done.8.refs_1_ = bf16[128,1024]{1,0:T(8,128)(2,1)S(1)} collective-permute-done((bf16[128,1024]{1,0:T(8,128)(2,1)S(1)}, bf16[128,1024]{1,0:T(8,128)(2,1)S(1)}, u32[]{:S(2)}, u32[]{:S(2)}) %collective-permute-start.8) | collective-permute-done | bytes 262176 | tf_op jit(solution)/shard_map/ppermute | solution.py:947
  108.5 2.9 %collective-permute-start.12 = (bf16[128,1024]{1,0:T(8,128)(2,1)S(1)}, bf16[128,1024]{1,0:T(8,128)(2,1)S(1)}, u32[]{:S(2)}, u32[]{:S(2)}) collective-permute-start(bf16[128,1024]{1,0:T(8,128)(2,1)S(1)} %add.18.refs_2_.refs_0_), channel_id=1, source_target_pairs={{0,16},{1,17},{2,18},{3,19},{4,20},{5,21},{6,22},{7,23},{8,24},{9,... | collective-permute-start | bytes 786440 | tf_op jit(solution)/shard_map/ppermute | solution.py:947
  111.3 6.5 %collective-permute-done.6.refs_1_ = bf16[64,2048]{1,0:T(8,128)(2,1)S(1)} collective-permute-done((bf16[64,2048]{1,0:T(8,128)(2,1)S(1)}, bf16[64,2048]{1,0:T(8,128)(2,1)S(1)}, u32[]{:S(2)}, u32[]{:S(2)}) %collective-permute-start.6) | collective-permute-done | bytes 262176 | tf_op jit(solution)/shard_map/ppermute | solution.py:947
  118.3 2.8 %collective-permute-start.17 = (bf16[64,2048]{1,0:T(8,128)(2,1)S(1)}, bf16[64,2048]{1,0:T(8,128)(2,1)S(1)}, u32[]{:S(2)}, u32[]{:S(2)}) collective-permute-start(bf16[64,2048]{1,0:T(8,128)(2,1)S(1)} %add.19.refs_4_.refs_0_), channel_id=1, source_target_pairs={{0,16},{1,17},{2,18},{3,19},{4,20},{5,21},{6,22},{7,23},{8,24},{9,... | collective-permute-start | bytes 786440 | tf_op jit(solution)/shard_map/ppermute | solution.py:947
  124.7 5.2 %collective-permute-done.12.refs_1_ = bf16[128,1024]{1,0:T(8,128)(2,1)S(1)} collective-permute-done((bf16[128,1024]{1,0:T(8,128)(2,1)S(1)}, bf16[128,1024]{1,0:T(8,128)(2,1)S(1)}, u32[]{:S(2)}, u32[]{:S(2)}) %collective-permute-start.12) | collective-permute-done | bytes 262176 | tf_op jit(solution)/shard_map/ppermute | solution.py:947
  137.7 3.2 %images_back.1 = (bf16[584,1024]{1,0:T(8,128)(2,1)}, f32[16,1024]{1,0:T(8,128)S(1)}) custom-call(bf16[584,1024]{1,0:T(8,128)(2,1)S(1)} %bitcast.13, bf16[1024]{0:T(1024)(128)(2,1)S(1)} %copy-done.28, f32[584,1024]{1,0:T(8,128)S(1)} %get-tuple-element.118.refs_5_.refs_2_, bf16[584,1024]{1,0:T(8,128)(2,1)S(1)} %back_in.1.refs_5_.refs_3_, ...), custom_call_target="tpu_custom_call" | custom-call | bytes 3000 | tf_op jit(solution)/shard_map/images_back/pallas_call | solution.py:308
  140.8 4.2 %collective-permute-done.14.refs_3_.refs_4_ = bf16[512,512]{1,0:T(8,128)(2,1)S(1)} collective-permute-done((bf16[512,512]{1,0:T(8,128)(2,1)S(1)}, bf16[512,512]{1,0:T(8,128)(2,1)S(1)}, u32[]{:S(2)}, u32[]{:S(2)}) %collective-permute-start.14) | collective-permute-done | bytes 524320 | tf_op jit(solution)/shard_map/ppermute | solution.py:947
  147.1 4.3 %collective-permute-done.23.refs_3_.refs_4_ = bf16[256,1024]{1,0:T(8,128)(2,1)S(1)} collective-permute-done((bf16[256,1024]{1,0:T(8,128)(2,1)S(1)}, bf16[256,1024]{1,0:T(8,128)(2,1)S(1)}, u32[]{:S(2)}, u32[]{:S(2)}) %collective-permute-start.23) | collective-permute-done | bytes 524320 | tf_op jit(solution)/shard_map/ppermute | solution.py:947
  151.3 3.8 %collective-permute-start.26 = (bf16[128,1024]{1,0:T(8,128)(2,1)S(1)}, bf16[128,1024]{1,0:T(8,128)(2,1)S(1)}, u32[]{:S(2)}, u32[]{:S(2)}) collective-permute-start(bf16[128,1024]{1,0:T(8,128)(2,1)S(1)} %add.20.refs_5_.refs_1_), channel_id=1, source_target_pairs={{0,8},{1,9},{2,10},{3,11},{4,12},{5,13},{6,14},{7,15},{8,0},{9,1},... | collective-permute-start | bytes 786440 | tf_op jit(solution)/shard_map/ppermute | solution.py:947
  159.6 3.4 %collective-permute-start.28 = (bf16[64,2048]{1,0:T(8,128)(2,1)S(1)}, bf16[64,2048]{1,0:T(8,128)(2,1)S(1)}, u32[]{:S(2)}, u32[]{:S(2)}) collective-permute-start(bf16[64,2048]{1,0:T(8,128)(2,1)S(1)} %add.22.refs_5_.refs_0_), channel_id=1, source_target_pairs={{0,16},{1,17},{2,18},{3,19},{4,20},{5,21},{6,22},{7,23},{8,24},{9,... | collective-permute-start | bytes 786440 | tf_op jit(solution)/shard_map/ppermute | solution.py:947
  165.2 3.1 %collective-permute-done.25.refs_1_ = f32[16,1024]{1,0:T(8,128)S(1)} collective-permute-done((f32[16,1024]{1,0:T(8,128)S(1)}, f32[16,1024]{1,0:T(8,128)S(1)}, u32[]{:S(2)}, u32[]{:S(2)}) %collective-permute-start.25) | collective-permute-done | bytes 65568 | tf_op jit(solution)/shard_map/ppermute | solution.py:1068
  168.3 3.8 %collective-permute-done.28.refs_1_ = bf16[64,2048]{1,0:T(8,128)(2,1)S(1)} collective-permute-done((bf16[64,2048]{1,0:T(8,128)(2,1)S(1)}, bf16[64,2048]{1,0:T(8,128)(2,1)S(1)}, u32[]{:S(2)}, u32[]{:S(2)}) %collective-permute-start.28) | collective-permute-done | bytes 262176 | tf_op jit(solution)/shard_map/ppermute | solution.py:947
  180.5 3.9 %collective-permute-done.32.refs_2_ = bf16[64,2048]{1,0:T(8,128)(2,1)S(1)} collective-permute-done((bf16[64,2048]{1,0:T(8,128)(2,1)S(1)}, bf16[64,2048]{1,0:T(8,128)(2,1)S(1)}, u32[]{:S(2)}, u32[]{:S(2)}) %collective-permute-start.32) | collective-permute-done | bytes 262176 | tf_op jit(solution)/shard_map/ppermute | solution.py:947
  194.1 8.3 %collective-permute-done.36.refs_1_ = bf16[256,512]{1,0:T(8,128)(2,1)S(1)} collective-permute-done((bf16[256,512]{1,0:T(8,128)(2,1)S(1)}, bf16[256,512]{1,0:T(8,128)(2,1)S(1)}, u32[]{:S(2)}, u32[]{:S(2)}) %collective-permute-start.36) | collective-permute-done | bytes 262176 | tf_op jit(solution)/shard_map/ppermute | solution.py:947
  224.1 5.2 %collective-permute-done.40.refs_2_ = bf16[512,512]{1,0:T(8,128)(2,1)S(1)} collective-permute-done((bf16[512,512]{1,0:T(8,128)(2,1)S(1)}, bf16[512,512]{1,0:T(8,128)(2,1)S(1)}, u32[]{:S(2)}, u32[]{:S(2)}) %collective-permute-start.40) | collective-permute-done | bytes 524320 | tf_op jit(solution)/shard_map/ppermute | solution.py:947
  245.1 16.7 %collective-permute-done.45.refs_1_ = bf16[256,2048]{1,0:T(8,128)(2,1)S(1)} collective-permute-done((bf16[256,2048]{1,0:T(8,128)(2,1)S(1)}, bf16[256,2048]{1,0:T(8,128)(2,1)S(1)}, u32[]{:S(2)}, u32[]{:S(2)}) %collective-permute-start.45) | collective-permute-done | bytes 1048608 | tf_op jit(solution)/shard_map/ppermute | solution.py:947
  (204 shorter events, 120.6 us)
Async XLA Ops:
  49.5 19.2 %collective-permute-start.3 = (bf16[256,2048]{1,0:T(8,128)(2,1)}, bf16[256,2048]{1,0:T(8,128)(2,1)S(1)}, u32[]{:S(2)}, u32[]{:S(2)}) collective-permute-start(bf16[256,2048]{1,0:T(8,128)(2,1)} %get-tuple-element.117), channel_id=1, source_target_pairs={{0,8},{1,5},{2,10},{3,7},{4,12},{5,1},{6,14},{7,3},{8,0},{9,13},{1... | collective-permute-start | bytes 3145736 | tf_op jit(solution)/shard_map/ppermute | solution.py:947
  52.2 32.4 %collective-permute-start.5 = (bf16[512,1024]{1,0:T(8,128)(2,1)}, bf16[512,1024]{1,0:T(8,128)(2,1)S(1)}, u32[]{:S(2)}, u32[]{:S(2)}) collective-permute-start(bf16[512,1024]{1,0:T(8,128)(2,1)} %get-tuple-element.124), channel_id=1, source_target_pairs={{0,2},{1,5},{2,0},{3,7},{4,6},{5,1},{6,4},{7,3},{8,10},{9,13},{10,... | collective-permute-start | bytes 3145736 | tf_op jit(solution)/shard_map/ppermute | solution.py:947
  60.7 38.6 %collective-permute-start.10 = (bf16[512,1024]{1,0:T(8,128)(2,1)}, bf16[512,1024]{1,0:T(8,128)(2,1)S(1)}, u32[]{:S(2)}, u32[]{:S(2)}) collective-permute-start(bf16[512,1024]{1,0:T(8,128)(2,1)} %get-tuple-element.135), channel_id=1, source_target_pairs={{0,2},{1,9},{2,0},{3,11},{4,6},{5,13},{6,4},{7,15},{8,10},{9,1},{1... | collective-permute-start | bytes 3145736 | tf_op jit(solution)/shard_map/ppermute | solution.py:947
  70.3 17.9 %collective-permute-start.4 = (bf16[128,2048]{1,0:T(8,128)(2,1)}, bf16[128,2048]{1,0:T(8,128)(2,1)S(1)}, u32[]{:S(2)}, u32[]{:S(2)}) collective-permute-start(bf16[128,2048]{1,0:T(8,128)(2,1)} %get-tuple-element.119.refs_6_), channel_id=1, source_target_pairs={{0,4},{1,3},{2,6},{3,1},{4,0},{5,7},{6,2},{7,5},{8,12},{9,11},{10,... | collective-permute-start | bytes 1572872 | tf_op jit(solution)/shard_map/ppermute | solution.py:947
  72.0 29.1 %collective-permute-start.9 = (bf16[256,2048]{1,0:T(8,128)(2,1)}, bf16[256,2048]{1,0:T(8,128)(2,1)S(1)}, u32[]{:S(2)}, u32[]{:S(2)}) collective-permute-start(bf16[256,2048]{1,0:T(8,128)(2,1)} %get-tuple-element.133), channel_id=1, source_target_pairs={{0,4},{1,9},{2,6},{3,11},{4,0},{5,13},{6,2},{7,15},{8,12},{9,1},{1... | collective-permute-start | bytes 3145736 | tf_op jit(solution)/shard_map/ppermute | solution.py:947
  88.1 30.2 %collective-permute-start.13 = (bf16[1024,512]{1,0:T(8,128)(2,1)}, bf16[1024,512]{1,0:T(8,128)(2,1)S(1)}, u32[]{:S(2)}, u32[]{:S(2)}) collective-permute-start(bf16[1024,512]{1,0:T(8,128)(2,1)} %get-tuple-element.140), channel_id=1, source_target_pairs={{0,4},{1,9},{2,6},{3,11},{4,0},{5,13},{6,2},{7,15},{8,12},{9,1},{1... | collective-permute-start | bytes 3145736 | tf_op jit(solution)/shard_map/ppermute | solution.py:947
  88.2 41.8 %collective-permute-start.11 = (bf16[1024,512]{1,0:T(8,128)(2,1)}, bf16[1024,512]{1,0:T(8,128)(2,1)S(1)}, u32[]{:S(2)}, u32[]{:S(2)}) collective-permute-start(bf16[1024,512]{1,0:T(8,128)(2,1)} %get-tuple-element.125.refs_5_), channel_id=1, source_target_pairs={{0,2},{1,3},{2,0},{3,1},{4,6},{5,7},{6,4},{7,5},{8,10},{9,11},{10,... | collective-permute-start | bytes 3145736 | tf_op jit(solution)/shard_map/ppermute | solution.py:947
  98.6 38.3 %collective-permute-start.15 = (bf16[584,1024]{1,0:T(8,128)(2,1)S(1)}, bf16[584,1024]{1,0:T(8,128)(2,1)S(1)}, u32[]{:S(2)}, u32[]{:S(2)}) collective-permute-start(bf16[584,1024]{1,0:T(8,128)(2,1)S(1)} %back_in.1.refs_5_.refs_3_), channel_id=1, source_target_pairs={{0,1},{1,0},{2,3},{3,2},{4,5},{5,4},{6,7},{7,6},{8,9},{9,8},{10,11... | collective-permute-start | bytes 3588104 | tf_op jit(solution)/shard_map/ppermute | solution.py:1013
  108.5 21.4 %collective-permute-start.12 = (bf16[128,1024]{1,0:T(8,128)(2,1)S(1)}, bf16[128,1024]{1,0:T(8,128)(2,1)S(1)}, u32[]{:S(2)}, u32[]{:S(2)}) collective-permute-start(bf16[128,1024]{1,0:T(8,128)(2,1)S(1)} %add.18.refs_2_.refs_0_), channel_id=1, source_target_pairs={{0,16},{1,17},{2,18},{3,19},{4,20},{5,21},{6,22},{7,23},{8,24},{9,... | collective-permute-start | bytes 786440 | tf_op jit(solution)/shard_map/ppermute | solution.py:947
  117.8 17.8 %collective-permute-start.16 = (bf16[128,2048]{1,0:T(8,128)(2,1)S(1)}, bf16[128,2048]{1,0:T(8,128)(2,1)S(1)}, u32[]{:S(2)}, u32[]{:S(2)}) collective-permute-start(bf16[128,2048]{1,0:T(8,128)(2,1)S(1)} %get-tuple-element.137.refs_2_), channel_id=1, source_target_pairs={{0,2},{1,5},{2,0},{3,7},{4,6},{5,1},{6,4},{7,3},{8,10},{9,13},{10,... | collective-permute-start | bytes 1572872 | tf_op jit(solution)/shard_map/ppermute | solution.py:947
  132.6 18.7 %collective-permute-start.23 = (bf16[256,1024]{1,0:T(8,128)(2,1)S(1)}, bf16[256,1024]{1,0:T(8,128)(2,1)S(1)}, u32[]{:S(2)}, u32[]{:S(2)}) collective-permute-start(bf16[256,1024]{1,0:T(8,128)(2,1)S(1)} %get-tuple-element.136.refs_5_), channel_id=1, source_target_pairs={{0,4},{1,3},{2,6},{3,1},{4,0},{5,7},{6,2},{7,5},{8,12},{9,11},{10,... | collective-permute-start | bytes 1572872 | tf_op jit(solution)/shard_map/ppermute | solution.py:947
  134.0 25.6 %collective-permute-start.20 = (bf16[512,512]{1,0:T(8,128)(2,1)S(1)}, bf16[512,512]{1,0:T(8,128)(2,1)S(1)}, u32[]{:S(2)}, u32[]{:S(2)}) collective-permute-start(bf16[512,512]{1,0:T(8,128)(2,1)S(1)} %get-tuple-element.141.refs_2_), channel_id=1, source_target_pairs={{0,2},{1,5},{2,0},{3,7},{4,6},{5,1},{6,4},{7,3},{8,10},{9,13},{10,... | collective-permute-start | bytes 1572872 | tf_op jit(solution)/shard_map/ppermute | solution.py:947
  135.6 19.5 %collective-permute-start.22 = (bf16[64,2048]{1,0:T(8,128)(2,1)S(1)}, bf16[64,2048]{1,0:T(8,128)(2,1)S(1)}, u32[]{:S(2)}, u32[]{:S(2)}) collective-permute-start(bf16[64,2048]{1,0:T(8,128)(2,1)S(1)} %add.21.refs_5_.refs_1_), channel_id=1, source_target_pairs={{0,2},{1,9},{2,0},{3,11},{4,6},{5,13},{6,4},{7,15},{8,10},{9,1},{1... | collective-permute-start | bytes 786440 | tf_op jit(solution)/shard_map/ppermute | solution.py:947
  136.9 21.1 %collective-permute-start.21 = (bf16[64,2048]{1,0:T(8,128)(2,1)S(1)}, bf16[64,2048]{1,0:T(8,128)(2,1)S(1)}, u32[]{:S(2)}, u32[]{:S(2)}) collective-permute-start(bf16[64,2048]{1,0:T(8,128)(2,1)S(1)} %get-tuple-element.149.refs_9_), channel_id=1, source_target_pairs={{0,8},{1,3},{2,10},{3,1},{4,12},{5,7},{6,14},{7,5},{8,0},{9,11},{1... | collective-permute-start | bytes 786440 | tf_op jit(solution)/shard_map/ppermute | solution.py:947
  157.9 20.5 %collective-permute-start.34 = (bf16[128,2048]{1,0:T(8,128)(2,1)S(1)}, bf16[128,2048]{1,0:T(8,128)(2,1)S(1)}, u32[]{:S(2)}, u32[]{:S(2)}) collective-permute-start(bf16[128,2048]{1,0:T(8,128)(2,1)S(1)} %join.12.refs_2_.refs_1_), channel_id=1, source_target_pairs={{0,4},{1,3},{2,6},{3,1},{4,0},{5,7},{6,2},{7,5},{8,12},{9,11},{10,... | collective-permute-start | bytes 1572872 | tf_op jit(solution)/shard_map/ppermute | solution.py:947
  168.3 46.1 %collective-permute-start.1 = (bf16[584,1024]{1,0:T(8,128)(2,1)S(1)}, bf16[584,1024]{1,0:T(8,128)(2,1)S(1)}, u32[]{:S(2)}, u32[]{:S(2)}) collective-permute-start(bf16[584,1024]{1,0:T(8,128)(2,1)S(1)} %down.1.refs_10_.refs_4_), channel_id=1, source_target_pairs={{0,1},{1,0},{2,3},{3,2},{4,5},{5,4},{6,7},{7,6},{8,9},{9,8},{10,11... | collective-permute-start | bytes 3588104 | tf_op jit(solution)/shard_map/ppermute | solution.py:1013
  188.4 19.1 %collective-permute-start.30 = (bf16[128,1024]{1,0:T(8,128)(2,1)S(1)}, bf16[128,1024]{1,0:T(8,128)(2,1)S(1)}, u32[]{:S(2)}, u32[]{:S(2)}) collective-permute-start(bf16[128,1024]{1,0:T(8,128)(2,1)S(1)} %add.26.refs_3_.refs_0_), channel_id=1, source_target_pairs={{0,16},{1,17},{2,18},{3,19},{4,20},{5,21},{6,22},{7,23},{8,24},{9,... | collective-permute-start | bytes 786440 | tf_op jit(solution)/shard_map/ppermute | solution.py:947
  193.1 39.7 %collective-permute-start.43 = (bf16[512,1024]{1,0:T(8,128)(2,1)S(1)}, bf16[512,1024]{1,0:T(8,128)(2,1)S(1)}, u32[]{:S(2)}, u32[]{:S(2)}) collective-permute-start(bf16[512,1024]{1,0:T(8,128)(2,1)S(1)} %join.16.refs_2_.refs_1_), channel_id=1, source_target_pairs={{0,2},{1,5},{2,0},{3,7},{4,6},{5,1},{6,4},{7,3},{8,10},{9,13},{10,... | collective-permute-start | bytes 3145736 | tf_op jit(solution)/shard_map/ppermute | solution.py:947
  220.9 19.7 %collective-permute-start.47 = (bf16[256,1024]{1,0:T(8,128)(2,1)S(1)}, bf16[256,1024]{1,0:T(8,128)(2,1)S(1)}, u32[]{:S(2)}, u32[]{:S(2)}) collective-permute-start(bf16[256,1024]{1,0:T(8,128)(2,1)S(1)} %join.19.refs_2_.refs_1_), channel_id=1, source_target_pairs={{0,4},{1,3},{2,6},{3,1},{4,0},{5,7},{6,2},{7,5},{8,12},{9,11},{10,... | collective-permute-start | bytes 1572872 | tf_op jit(solution)/shard_map/ppermute | solution.py:947
  221.7 42.1 %collective-permute-start.44 = (bf16[256,2048]{1,0:T(8,128)(2,1)S(1)}, bf16[256,2048]{1,0:T(8,128)(2,1)S(1)}, u32[]{:S(2)}, u32[]{:S(2)}) collective-permute-start(bf16[256,2048]{1,0:T(8,128)(2,1)S(1)} %join.14.refs_2_.refs_1_), channel_id=1, source_target_pairs={{0,8},{1,5},{2,10},{3,7},{4,12},{5,1},{6,14},{7,3},{8,0},{9,13},{1... | collective-permute-start | bytes 3145736 | tf_op jit(solution)/shard_map/ppermute | solution.py:947
  229.3 32.4 %collective-permute-start.45 = (bf16[256,2048]{1,0:T(8,128)(2,1)S(1)}, bf16[256,2048]{1,0:T(8,128)(2,1)S(1)}, u32[]{:S(2)}, u32[]{:S(2)}) collective-permute-start(bf16[256,2048]{1,0:T(8,128)(2,1)S(1)} %join.17.refs_2_.refs_1_), channel_id=1, source_target_pairs={{0,4},{1,9},{2,6},{3,11},{4,0},{5,13},{6,2},{7,15},{8,12},{9,1},{1... | collective-permute-start | bytes 3145736 | tf_op jit(solution)/shard_map/ppermute | solution.py:947
  232.8 32.8 %collective-permute-start.42 = (bf16[1024,512]{1,0:T(8,128)(2,1)S(1)}, bf16[1024,512]{1,0:T(8,128)(2,1)S(1)}, u32[]{:S(2)}, u32[]{:S(2)}) collective-permute-start(bf16[1024,512]{1,0:T(8,128)(2,1)S(1)} %join.21.refs_2_.refs_1_), channel_id=1, source_target_pairs={{0,2},{1,3},{2,0},{3,1},{4,6},{5,7},{6,4},{7,5},{8,10},{9,11},{10,... | collective-permute-start | bytes 3145736 | tf_op jit(solution)/shard_map/ppermute | solution.py:947
  241.2 29.7 %collective-permute-start.49 = (bf16[512,1024]{1,0:T(8,128)(2,1)S(1)}, bf16[512,1024]{1,0:T(8,128)(2,1)S(1)}, u32[]{:S(2)}, u32[]{:S(2)}) collective-permute-start(bf16[512,1024]{1,0:T(8,128)(2,1)S(1)} %join.23.refs_1_.refs_3_), channel_id=1, source_target_pairs={{0,2},{1,9},{2,0},{3,11},{4,6},{5,13},{6,4},{7,15},{8,10},{9,1},{1... | collective-permute-start | bytes 3145736 | tf_op jit(solution)/shard_map/ppermute | solution.py:947
  242.1 30.9 %collective-permute-start.48 = (bf16[1024,512]{1,0:T(8,128)(2,1)S(1)}, bf16[1024,512]{1,0:T(8,128)(2,1)S(1)}, u32[]{:S(2)}, u32[]{:S(2)}) collective-permute-start(bf16[1024,512]{1,0:T(8,128)(2,1)S(1)} %join.22.refs_3_.refs_1_), channel_id=1, source_target_pairs={{0,4},{1,9},{2,6},{3,11},{4,0},{5,13},{6,2},{7,15},{8,12},{9,1},{1... | collective-permute-start | bytes 3145736 | tf_op jit(solution)/shard_map/ppermute | solution.py:947
  (58 other events, 439.8 us)

commit v2 on v1

--- a/solution.py
+++ b/solution.py
@@ -967,19 +967,19 @@
 
 
 ORDERS = {
-    "D0": ((0, 1, 2), (1, 0, 2)),
-    "D1": ((0, 1, 2), (2, 0, 1)),
-    "U0": ((2, 1, 0), (1, 0, 2)),
-    "U1": ((1, 0, 2), (2, 1, 0)),
+    "D0": ((1, 2, 0), (0, 2, 1)),
+    "D1": ((2, 0, 1), (1, 0, 2)),
+    "U0": ((2, 0, 1), (2, 1, 0)),
+    "U1": ((1, 0, 2), (0, 1, 2)),
     "Q0": ((0, 1, 2), (0, 1, 2)),
     "Q1": ((1, 0, 2), (2, 1, 0)),
 }
 SCHEDULE = (
-    "down", "resid_back", "U0", "attend_back", "q_send", "D0", "U0", "back_in", "D0", "D1", "U1", "D0",
-    "U0", "q_keep", "Q1", "D0", "Q0", "U0", "U1", "images_back", "Q0", "D1", "U0", "U1", "Q1", "pack0",
-    "Q0", "U1", "D1", "D0", "pack1", "Q0", "U0", "Q1", "U1", "U0", "D0", "Q1", "U1", "pack2", "D1",
-    "Q0", "block_out", "D1", "pack3", "Q1", "Q0", "D0", "D0", "Q0", "Q1", "U1", "D1", "D1", "U1", "U0",
-    "Q0", "unpack", "Q1", "D1", "Q1",
+    "resid_back", "attend_back", "q_send", "D1", "back_in", "U0", "D0", "q_keep", "D1", "U0", "U1",
+    "D1", "Q1", "D0", "Q0", "U1", "D1", "D0", "images_back", "U1", "D0", "Q0", "Q1", "U1", "U0",
+    "pack0", "Q1", "D1", "U1", "D0", "U0", "pack1", "Q1", "Q0", "U0", "pack2", "D1", "Q1", "Q0", "U1",
+    "down", "Q0", "U0", "Q1", "D0", "D0", "D1", "D1", "pack3", "U1", "D0", "Q0", "Q1", "U0", "unpack",
+    "Q0", "U1", "block_out", "U0", "Q0", "Q1",
 )
 
 

time: 280 us -> 263 us (0.939)
  waiting for transfers between devices: 82 us -> 67.5 us
    ppermute x42, waiting for transfers between devices: 74.5 us -> 55.6 us  [over(): return lax.ppermute(piece, ('dp', 'tensor'), pairs)]
    ppermute x4, waiting for transfers between devices: 5.38 us -> 9.75 us  [compute(): lax.ppermute(have['pack'], 'dp', xor_pairs(1 << int(name[4])))]
  transfers between devices with their start and end apart: 50 -> 50, of which waited for: 21 -> 19; matrix products, arithmetic and copies ran while one was open for 0% -> 0% of each run, Pallas kernels for 26% -> 27%
where the time goes in v2:
time: 263 us; the launch traced here: 260 us
  Pallas kernels  117 us (44%)
  waiting for transfers between devices  67.5 us (26%)
  starting transfers between devices  62 us (24%)
  local copies, waits for them, and re-layouts  10.5 us (4%)
    pallas_call x63, Pallas kernels, __call__(): pl.pallas_call(run, out_shape=outs, grid_spec=spec, input_output_aliases=...  117 us
    ppermute x42, starting transfers between devices, over(): return lax.ppermute(piece, ('dp', 'tensor'), pairs)  58.4 us
    ppermute x42, waiting for transfers between devices, over(): return lax.ppermute(piece, ('dp', 'tensor'), pairs)  55.6 us
    unnamed x64, local copies, waits for them, and re-layouts  10.5 us
    ppermute x4, waiting for transfers between devices, compute(): lax.ppermute(have['pack'], 'dp', xor_pairs(1 << int(name[4])))  9.75 us
  transfers between devices with their start and end apart: 50, of which 19 were waited for; matrix products, arithmetic and copies ran while one was open for 0% of the time, Pallas kernels for 27%

profile of v2, /device:TPU:0, one launch (start us, length us, event | category | flops | bytes accessed | tf_op | source)
XLA Modules:
  0.0 259.7 jit_solution(14250079679617804533)
XLA Ops:
  1.3 18.2 %attend.1 = (bf16[584,1024]{1,0:T(8,128)(2,1)}, bf16[592,512]{1,0:T(8,128)(2,1)}, bf16[592,512]{1,0:T(8,128)(2,1)}, bf16[592,512]{1,0:T(8,128)(2,1)}, bf16[592,5...) custom-call(s32[1]{0:T(128)S(6)} %copy.49.mask_ref, ...), custom_call_target="tpu_custom_call" | custom-call | bytes 3000 | tf_op jit(solution)/shard_map/attend/pallas_call | solution.py:308
  23.8 25.5 %feed.1 = (bf16[584,2048]{1,0:T(8,128)(2,1)}, bf16[584,1024]{1,0:T(8,128)(2,1)}, bf16[512,1024]{1,0:T(8,128)(2,1)}, bf16[512,1024]{1,0:T(8,128)(2,1)}, bf16[512,...) custom-call(s32[2]{0:T(128)} %pad_add_fusion.refs_0_, ...), custom_call_target="tpu_custom_call" | custom-call | bytes 3000 | tf_op jit(solution)/shard_map/feed/pallas_call | solution.py:308
  49.7 2.7 %collective-permute-start.4 = (bf16[512,1024]{1,0:T(8,128)(2,1)}, bf16[512,1024]{1,0:T(8,128)(2,1)S(1)}, u32[]{:S(2)}, u32[]{:S(2)}) collective-permute-start(bf16[512,1024]{1,0:T(8,128)(2,1)} %get-tuple-element.122), channel_id=1, source_target_pairs={{0,8},{1,5},{2,10},{3,7},{4,12},{5,1},{6,14},{7,3},{8,0},{9,13},{1... | collective-permute-start | bytes 3145736 | tf_op jit(solution)/shard_map/ppermute | solution.py:947
  60.6 3.8 %resid_back.1 = (f32[584,1024]{1,0:T(8,128)S(1)}, bf16[592,512]{1,0:T(8,128)(2,1)S(1)}, f32[8,1024]{1,0:T(8,128)S(1)}, bf16[1024,512]{1,0:T(8,128)(2,1)S(1)}) custom-call(bf16[584,1024]{1,0:T(8,128)(2,1)S(1)} %bitcast.12, bf16[584,1024]{1,0:T(8,128)(2,1)S(1)} %copy-done.1, bf16[584,1024]{1,0:T(8,128)(2,1)S(1)} %copy-done.5, bf16[1024]{0:T(1024)(128)(2,1)S(1)} %copy-done.25, ...), custom_call_target="tpu_custom_call" | custom-call | bytes 3000 | tf_op jit(solution)/shard_map/resid_back/pallas_call | solution.py:308
  64.5 9.2 %attend_back.1 = (bf16[592,1536]{1,0:T(8,128)(2,1)S(1)}, f32[1,1536]{1,0:T(1,128)S(1)}) custom-call(bf16[592,512]{1,0:T(8,128)(2,1)S(1)} %copy-done.21, bf16[592,512]{1,0:T(8,128)(2,1)S(1)} %copy-done.22, bf16[592,512]{1,0:T(8,128)(2,1)S(1)} %copy-done.23, bf16[592,512]{1,0:T(8,128)(2,1)S(1)} %copy-done.17, bf16[592,512]{1,0:T(8,128)(2,1)S(1)} %get-tuple-element.117.refs_4_, ...), custom_call_target="tpu_custom_call" | custom-call | bytes 3000 | tf_op jit(solution)/shard_map/attend_back/pallas_call | solution.py:308
  73.7 2.9 %qkv_grad.2 = (bf16[1024,512]{1,0:T(8,128)(2,1)}, bf16[1024,512]{1,0:T(8,128)(2,1)}) custom-call(s32[2]{0:T(128)S(1)} %copy-done.20, bf16[592,1024]{1,0:T(8,128)(2,1)S(1)} %copy-done.8, bf16[592,1536]{1,0:T(8,128)(2,1)S(1)} %get-tuple-element.120.refs_2_.refs_4_.refs_0_, bf16[1024,512]{1,0:T(8,128)(2,1)S(1)} %get-tuple-element.124.refs_3_, ...), custom_call_target="tpu_custom_call" | custom-call | bytes 3000 | tf_op jit(solution)/shard_map/qkv_grad/pallas_call | solution.py:308
  82.6 5.0 %back_in.1.refs_5_.refs_3_ = bf16[584,1024]{1,0:T(8,128)(2,1)S(1)} custom-call(bf16[592,1536]{1,0:T(8,128)(2,1)S(1)} %get-tuple-element.120.refs_2_.refs_4_.refs_0_, bf16[3,1024,512]{2,1,0:T(8,128)(2,1)S(1)} %bitcast.16, bf16[256,1024]{1,0:T(8,128)(2,1)} %get-tuple-element.126.refs_2_), custom_call_target="tpu_custom_call" | custom-call | bytes 3000 | tf_op jit(solution)/shard_map/back_in/pallas_call | solution.py:308
  87.6 5.4 %collective-permute-done.2.refs_3_.refs_4_ = bf16[256,2048]{1,0:T(8,128)(2,1)S(1)} collective-permute-done((bf16[256,2048]{1,0:T(8,128)(2,1)}, bf16[256,2048]{1,0:T(8,128)(2,1)S(1)}, u32[]{:S(2)}, u32[]{:S(2)}) %collective-permute-start.2) | collective-permute-done | bytes 1048608 | tf_op jit(solution)/shard_map/ppermute | solution.py:947
  93.7 3.1 %collective-permute-start.5 = (bf16[128,2048]{1,0:T(8,128)(2,1)S(1)}, bf16[128,2048]{1,0:T(8,128)(2,1)S(1)}, u32[]{:S(2)}, u32[]{:S(2)}) collective-permute-start(bf16[128,2048]{1,0:T(8,128)(2,1)S(1)} %get-tuple-element.128.refs_5_), channel_id=1, source_target_pairs={{0,2},{1,5},{2,0},{3,7},{4,6},{5,1},{6,4},{7,3},{8,10},{9,13},{10,... | collective-permute-start | bytes 1572872 | tf_op jit(solution)/shard_map/ppermute | solution.py:947
  101.6 8.1 %collective-permute-done.5.refs_3_.refs_4_ = bf16[128,2048]{1,0:T(8,128)(2,1)S(1)} collective-permute-done((bf16[128,2048]{1,0:T(8,128)(2,1)S(1)}, bf16[128,2048]{1,0:T(8,128)(2,1)S(1)}, u32[]{:S(2)}, u32[]{:S(2)}) %collective-permute-start.5) | collective-permute-done | bytes 524320 | tf_op jit(solution)/shard_map/ppermute | solution.py:947
  117.8 3.8 %collective-permute-done.10.refs_3_.refs_4_ = bf16[256,1024]{1,0:T(8,128)(2,1)S(1)} collective-permute-done((bf16[256,1024]{1,0:T(8,128)(2,1)S(1)}, bf16[256,1024]{1,0:T(8,128)(2,1)S(1)}, u32[]{:S(2)}, u32[]{:S(2)}) %collective-permute-start.10) | collective-permute-done | bytes 524320 | tf_op jit(solution)/shard_map/ppermute | solution.py:947
  133.1 3.2 %images_back.1 = (bf16[584,1024]{1,0:T(8,128)(2,1)}, f32[16,1024]{1,0:T(8,128)S(1)}) custom-call(bf16[584,1024]{1,0:T(8,128)(2,1)S(1)} %bitcast.13, bf16[1024]{0:T(1024)(128)(2,1)S(1)} %copy-done.28, f32[584,1024]{1,0:T(8,128)S(1)} %get-tuple-element.119.refs_6_.refs_2_, bf16[584,1024]{1,0:T(8,128)(2,1)S(1)} %back_in.1.refs_5_.refs_3_, ...), custom_call_target="tpu_custom_call" | custom-call | bytes 3000 | tf_op jit(solution)/shard_map/images_back/pallas_call | solution.py:308
  137.6 3.3 %collective-permute-start.17 = (bf16[64,2048]{1,0:T(8,128)(2,1)S(1)}, bf16[64,2048]{1,0:T(8,128)(2,1)S(1)}, u32[]{:S(2)}, u32[]{:S(2)}) collective-permute-start(bf16[64,2048]{1,0:T(8,128)(2,1)S(1)} %add.21.refs_2_.refs_0_), channel_id=1, source_target_pairs={{0,16},{1,17},{2,18},{3,19},{4,20},{5,21},{6,22},{7,23},{8,24},{9,... | collective-permute-start | bytes 786440 | tf_op jit(solution)/shard_map/ppermute | solution.py:947
  153.2 3.9 %collective-permute-start.30 = (bf16[64,2048]{1,0:T(8,128)(2,1)S(1)}, bf16[64,2048]{1,0:T(8,128)(2,1)S(1)}, u32[]{:S(2)}, u32[]{:S(2)}) collective-permute-start(bf16[64,2048]{1,0:T(8,128)(2,1)S(1)} %add.24.refs_2_.refs_0_), channel_id=1, source_target_pairs={{0,16},{1,17},{2,18},{3,19},{4,20},{5,21},{6,22},{7,23},{8,24},{9,... | collective-permute-start | bytes 786440 | tf_op jit(solution)/shard_map/ppermute | solution.py:947
  161.5 8.5 %collective-permute-done.21.refs_2_ = bf16[64,2048]{1,0:T(8,128)(2,1)S(1)} collective-permute-done((bf16[64,2048]{1,0:T(8,128)(2,1)S(1)}, bf16[64,2048]{1,0:T(8,128)(2,1)S(1)}, u32[]{:S(2)}, u32[]{:S(2)}) %collective-permute-start.21) | collective-permute-done | bytes 262176 | tf_op jit(solution)/shard_map/ppermute | solution.py:947
  177.1 3.2 %collective-permute-done.27.refs_1_ = bf16[256,512]{1,0:T(8,128)(2,1)S(1)} collective-permute-done((bf16[256,512]{1,0:T(8,128)(2,1)S(1)}, bf16[256,512]{1,0:T(8,128)(2,1)S(1)}, u32[]{:S(2)}, u32[]{:S(2)}) %collective-permute-start.27) | collective-permute-done | bytes 262176 | tf_op jit(solution)/shard_map/ppermute | solution.py:947
  181.8 8.3 %collective-permute-done.35.refs_1_ = f32[16,1024]{1,0:T(8,128)S(1)} collective-permute-done((f32[16,1024]{1,0:T(8,128)S(1)}, f32[16,1024]{1,0:T(8,128)S(1)}, u32[]{:S(2)}, u32[]{:S(2)}) %collective-permute-start.35) | collective-permute-done | bytes 65568 | tf_op jit(solution)/shard_map/ppermute | solution.py:1068
  196.4 3.0 %down.1.refs_3_.refs_4_ = bf16[584,1024]{1,0:T(8,128)(2,1)S(1)} custom-call(bf16[584,2048]{1,0:T(8,128)(2,1)S(1)} %copy-done.7, bf16[2048,1024]{1,0:T(8,128)(2,1)S(1)} %copy-done.2, bf16[256,2048]{1,0:T(8,128)(2,1)S(1)} %join.18.refs_2_.refs_1_), custom_call_target="tpu_custom_call" | custom-call | bytes 3000 | tf_op jit(solution)/shard_map/down/pallas_call | solution.py:308
  199.4 6.1 %collective-permute-done.40.refs_2_ = bf16[256,512]{1,0:T(8,128)(2,1)S(1)} collective-permute-done((bf16[256,512]{1,0:T(8,128)(2,1)S(1)}, bf16[256,512]{1,0:T(8,128)(2,1)S(1)}, u32[]{:S(2)}, u32[]{:S(2)}) %collective-permute-start.40) | collective-permute-done | bytes 262176 | tf_op jit(solution)/shard_map/ppermute | solution.py:947
  206.7 3.3 %collective-permute-done.44.refs_2_ = bf16[512,512]{1,0:T(8,128)(2,1)S(1)} collective-permute-done((bf16[512,512]{1,0:T(8,128)(2,1)S(1)}, bf16[512,512]{1,0:T(8,128)(2,1)S(1)}, u32[]{:S(2)}, u32[]{:S(2)}) %collective-permute-start.44) | collective-permute-done | bytes 524320 | tf_op jit(solution)/shard_map/ppermute | solution.py:947
  211.2 3.4 %collective-permute-start.46 = (bf16[512,1024]{1,0:T(8,128)(2,1)S(1)}, bf16[512,1024]{1,0:T(8,128)(2,1)S(1)}, u32[]{:S(2)}, u32[]{:S(2)}) collective-permute-start(bf16[512,1024]{1,0:T(8,128)(2,1)S(1)} %join.22.refs_1_.refs_2_), channel_id=1, source_target_pairs={{0,4},{1,3},{2,6},{3,1},{4,0},{5,7},{6,2},{7,5},{8,12},{9,11},{10,... | collective-permute-start | bytes 3145736 | tf_op jit(solution)/shard_map/ppermute | solution.py:947
  224.7 2.8 %collective-permute-done.46.refs_1_ = bf16[512,1024]{1,0:T(8,128)(2,1)S(1)} collective-permute-done((bf16[512,1024]{1,0:T(8,128)(2,1)S(1)}, bf16[512,1024]{1,0:T(8,128)(2,1)S(1)}, u32[]{:S(2)}, u32[]{:S(2)}) %collective-permute-start.46) | collective-permute-done | bytes 1048608 | tf_op jit(solution)/shard_map/ppermute | solution.py:947
  229.4 3.7 %collective-permute-done.45.refs_2_ = bf16[512,512]{1,0:T(8,128)(2,1)S(1)} collective-permute-done((bf16[512,512]{1,0:T(8,128)(2,1)S(1)}, bf16[512,512]{1,0:T(8,128)(2,1)S(1)}, u32[]{:S(2)}, u32[]{:S(2)}) %collective-permute-start.45) | collective-permute-done | bytes 524320 | tf_op jit(solution)/shard_map/ppermute | solution.py:947
  252.0 3.5 %collective-permute-done.48.refs_1_ = bf16[1024,512]{1,0:T(8,128)(2,1)S(1)} collective-permute-done((bf16[1024,512]{1,0:T(8,128)(2,1)S(1)}, bf16[1024,512]{1,0:T(8,128)(2,1)S(1)}, u32[]{:S(2)}, u32[]{:S(2)}) %collective-permute-start.48) | collective-permute-done | bytes 1048608 | tf_op jit(solution)/shard_map/ppermute | solution.py:947
  (204 shorter events, 113.3 us)
Async XLA Ops:
  49.7 27.0 %collective-permute-start.4 = (bf16[512,1024]{1,0:T(8,128)(2,1)}, bf16[512,1024]{1,0:T(8,128)(2,1)S(1)}, u32[]{:S(2)}, u32[]{:S(2)}) collective-permute-start(bf16[512,1024]{1,0:T(8,128)(2,1)} %get-tuple-element.122), channel_id=1, source_target_pairs={{0,8},{1,5},{2,10},{3,7},{4,12},{5,1},{6,14},{7,3},{8,0},{9,13},{1... | collective-permute-start | bytes 3145736 | tf_op jit(solution)/shard_map/ppermute | solution.py:947
  52.4 40.6 %collective-permute-start.2 = (bf16[256,2048]{1,0:T(8,128)(2,1)}, bf16[256,2048]{1,0:T(8,128)(2,1)S(1)}, u32[]{:S(2)}, u32[]{:S(2)}) collective-permute-start(bf16[256,2048]{1,0:T(8,128)(2,1)} %get-tuple-element.111), channel_id=1, source_target_pairs={{0,8},{1,9},{2,10},{3,11},{4,12},{5,13},{6,14},{7,15},{8,0},{9,1},... | collective-permute-start | bytes 3145736 | tf_op jit(solution)/shard_map/ppermute | solution.py:947
  52.4 44.5 %collective-permute-start.7 = (bf16[512,1024]{1,0:T(8,128)(2,1)}, bf16[512,1024]{1,0:T(8,128)(2,1)S(1)}, u32[]{:S(2)}, u32[]{:S(2)}) collective-permute-start(bf16[512,1024]{1,0:T(8,128)(2,1)} %get-tuple-element.131), channel_id=1, source_target_pairs={{0,4},{1,3},{2,6},{3,1},{4,0},{5,7},{6,2},{7,5},{8,12},{9,11},{10,... | collective-permute-start | bytes 3145736 | tf_op jit(solution)/shard_map/ppermute | solution.py:947
  54.3 47.3 %collective-permute-start.1 = (bf16[256,2048]{1,0:T(8,128)(2,1)}, bf16[256,2048]{1,0:T(8,128)(2,1)S(1)}, u32[]{:S(2)}, u32[]{:S(2)}) collective-permute-start(bf16[256,2048]{1,0:T(8,128)(2,1)} %get-tuple-element.109), channel_id=1, source_target_pairs={{0,4},{1,3},{2,6},{3,1},{4,0},{5,7},{6,2},{7,5},{8,12},{9,11},{10,... | collective-permute-start | bytes 3145736 | tf_op jit(solution)/shard_map/ppermute | solution.py:947
  78.2 22.3 %collective-permute-start.6 = (bf16[256,1024]{1,0:T(8,128)(2,1)}, bf16[256,1024]{1,0:T(8,128)(2,1)S(1)}, u32[]{:S(2)}, u32[]{:S(2)}) collective-permute-start(bf16[256,1024]{1,0:T(8,128)(2,1)} %get-tuple-element.126.refs_2_), channel_id=1, source_target_pairs={{0,2},{1,3},{2,0},{3,1},{4,6},{5,7},{6,4},{7,5},{8,10},{9,11},{10,... | collective-permute-start | bytes 1572872 | tf_op jit(solution)/shard_map/ppermute | solution.py:947
  80.1 34.2 %collective-permute-start.11 = (bf16[1024,512]{1,0:T(8,128)(2,1)}, bf16[1024,512]{1,0:T(8,128)(2,1)S(1)}, u32[]{:S(2)}, u32[]{:S(2)}) collective-permute-start(bf16[1024,512]{1,0:T(8,128)(2,1)} %get-tuple-element.140), channel_id=1, source_target_pairs={{0,4},{1,9},{2,6},{3,11},{4,0},{5,13},{6,2},{7,15},{8,12},{9,1},{1... | collective-permute-start | bytes 3145736 | tf_op jit(solution)/shard_map/ppermute | solution.py:947
  96.9 27.8 %collective-permute-start.9 = (bf16[1024,512]{1,0:T(8,128)(2,1)}, bf16[1024,512]{1,0:T(8,128)(2,1)S(1)}, u32[]{:S(2)}, u32[]{:S(2)}) collective-permute-start(bf16[1024,512]{1,0:T(8,128)(2,1)} %get-tuple-element.125.refs_5_), channel_id=1, source_target_pairs={{0,2},{1,3},{2,0},{3,1},{4,6},{5,7},{6,4},{7,5},{8,10},{9,11},{10,... | collective-permute-start | bytes 3145736 | tf_op jit(solution)/shard_map/ppermute | solution.py:947
  101.6 31.5 %collective-permute-start.14 = (bf16[584,1024]{1,0:T(8,128)(2,1)S(1)}, bf16[584,1024]{1,0:T(8,128)(2,1)S(1)}, u32[]{:S(2)}, u32[]{:S(2)}) collective-permute-start(bf16[584,1024]{1,0:T(8,128)(2,1)S(1)} %back_in.1.refs_5_.refs_3_), channel_id=1, source_target_pairs={{0,1},{1,0},{2,3},{3,2},{4,5},{5,4},{6,7},{7,6},{8,9},{9,8},{10,11... | collective-permute-start | bytes 3588104 | tf_op jit(solution)/shard_map/ppermute | solution.py:1013
  125.5 18.4 %collective-permute-start.19 = (bf16[512,512]{1,0:T(8,128)(2,1)S(1)}, bf16[512,512]{1,0:T(8,128)(2,1)S(1)}, u32[]{:S(2)}, u32[]{:S(2)}) collective-permute-start(bf16[512,512]{1,0:T(8,128)(2,1)S(1)} %get-tuple-element.144.refs_5_), channel_id=1, source_target_pairs={{0,4},{1,5},{2,6},{3,7},{4,0},{5,1},{6,2},{7,3},{8,12},{9,13},{10,... | collective-permute-start | bytes 1572872 | tf_op jit(solution)/shard_map/ppermute | solution.py:947
  127.4 17.1 %collective-permute-start.18 = (bf16[512,512]{1,0:T(8,128)(2,1)S(1)}, bf16[512,512]{1,0:T(8,128)(2,1)S(1)}, u32[]{:S(2)}, u32[]{:S(2)}) collective-permute-start(bf16[512,512]{1,0:T(8,128)(2,1)S(1)} %get-tuple-element.142.refs_5_), channel_id=1, source_target_pairs={{0,2},{1,5},{2,0},{3,7},{4,6},{5,1},{6,4},{7,3},{8,10},{9,13},{10,... | collective-permute-start | bytes 1572872 | tf_op jit(solution)/shard_map/ppermute | solution.py:947
  150.5 19.6 %collective-permute-start.21 = (bf16[64,2048]{1,0:T(8,128)(2,1)S(1)}, bf16[64,2048]{1,0:T(8,128)(2,1)S(1)}, u32[]{:S(2)}, u32[]{:S(2)}) collective-permute-start(bf16[64,2048]{1,0:T(8,128)(2,1)S(1)} %add.23.refs_2_.refs_1_), channel_id=1, source_target_pairs={{0,8},{1,9},{2,10},{3,11},{4,12},{5,13},{6,14},{7,15},{8,0},{9,1},... | collective-permute-start | bytes 786440 | tf_op jit(solution)/shard_map/ppermute | solution.py:947
  153.1 17.5 %collective-permute-start.31 = (bf16[128,1024]{1,0:T(8,128)(2,1)S(1)}, bf16[128,1024]{1,0:T(8,128)(2,1)S(1)}, u32[]{:S(2)}, u32[]{:S(2)}) collective-permute-start(bf16[128,1024]{1,0:T(8,128)(2,1)S(1)} %add.22.refs_5_.refs_1_), channel_id=1, source_target_pairs={{0,2},{1,5},{2,0},{3,7},{4,6},{5,1},{6,4},{7,3},{8,10},{9,13},{10,... | collective-permute-start | bytes 786440 | tf_op jit(solution)/shard_map/ppermute | solution.py:947
  153.2 18.1 %collective-permute-start.30 = (bf16[64,2048]{1,0:T(8,128)(2,1)S(1)}, bf16[64,2048]{1,0:T(8,128)(2,1)S(1)}, u32[]{:S(2)}, u32[]{:S(2)}) collective-permute-start(bf16[64,2048]{1,0:T(8,128)(2,1)S(1)} %add.24.refs_2_.refs_0_), channel_id=1, source_target_pairs={{0,16},{1,17},{2,18},{3,19},{4,20},{5,21},{6,22},{7,23},{8,24},{9,... | collective-permute-start | bytes 786440 | tf_op jit(solution)/shard_map/ppermute | solution.py:947
  159.3 30.9 %collective-permute-start.34 = (bf16[256,1024]{1,0:T(8,128)(2,1)S(1)}, bf16[256,1024]{1,0:T(8,128)(2,1)S(1)}, u32[]{:S(2)}, u32[]{:S(2)}) collective-permute-start(bf16[256,1024]{1,0:T(8,128)(2,1)S(1)} %join.12.refs_3_.refs_1_), channel_id=1, source_target_pairs={{0,2},{1,3},{2,0},{3,1},{4,6},{5,7},{6,4},{7,5},{8,10},{9,11},{10,... | collective-permute-start | bytes 1572872 | tf_op jit(solution)/shard_map/ppermute | solution.py:947
  191.4 18.6 %collective-permute-start.44 = (bf16[512,512]{1,0:T(8,128)(2,1)S(1)}, bf16[512,512]{1,0:T(8,128)(2,1)S(1)}, u32[]{:S(2)}, u32[]{:S(2)}) collective-permute-start(bf16[512,512]{1,0:T(8,128)(2,1)S(1)} %join.17.refs_2_.refs_1_), channel_id=1, source_target_pairs={{0,2},{1,5},{2,0},{3,7},{4,6},{5,1},{6,4},{7,3},{8,10},{9,13},{10,... | collective-permute-start | bytes 1572872 | tf_op jit(solution)/shard_map/ppermute | solution.py:947
  193.5 17.1 %collective-permute-start.43 = (bf16[256,1024]{1,0:T(8,128)(2,1)S(1)}, bf16[256,1024]{1,0:T(8,128)(2,1)S(1)}, u32[]{:S(2)}, u32[]{:S(2)}) collective-permute-start(bf16[256,1024]{1,0:T(8,128)(2,1)S(1)} %join.14.refs_2_.refs_1_), channel_id=1, source_target_pairs={{0,8},{1,9},{2,10},{3,11},{4,12},{5,13},{6,14},{7,15},{8,0},{9,1},... | collective-permute-start | bytes 1572872 | tf_op jit(solution)/shard_map/ppermute | solution.py:947
  195.7 23.0 %collective-permute-start.42 = (bf16[512,1024]{1,0:T(8,128)(2,1)S(1)}, bf16[512,1024]{1,0:T(8,128)(2,1)S(1)}, u32[]{:S(2)}, u32[]{:S(2)}) collective-permute-start(bf16[512,1024]{1,0:T(8,128)(2,1)S(1)} %join.16.refs_3_.refs_1_), channel_id=1, source_target_pairs={{0,8},{1,5},{2,10},{3,7},{4,12},{5,1},{6,14},{7,3},{8,0},{9,13},{1... | collective-permute-start | bytes 3145736 | tf_op jit(solution)/shard_map/ppermute | solution.py:947
  211.2 16.2 %collective-permute-start.46 = (bf16[512,1024]{1,0:T(8,128)(2,1)S(1)}, bf16[512,1024]{1,0:T(8,128)(2,1)S(1)}, u32[]{:S(2)}, u32[]{:S(2)}) collective-permute-start(bf16[512,1024]{1,0:T(8,128)(2,1)S(1)} %join.22.refs_1_.refs_2_), channel_id=1, source_target_pairs={{0,4},{1,3},{2,6},{3,1},{4,0},{5,7},{6,2},{7,5},{8,12},{9,11},{10,... | collective-permute-start | bytes 3145736 | tf_op jit(solution)/shard_map/ppermute | solution.py:947
  214.7 18.4 %collective-permute-start.45 = (bf16[512,512]{1,0:T(8,128)(2,1)S(1)}, bf16[512,512]{1,0:T(8,128)(2,1)S(1)}, u32[]{:S(2)}, u32[]{:S(2)}) collective-permute-start(bf16[512,512]{1,0:T(8,128)(2,1)S(1)} %join.19.refs_3_.refs_1_), channel_id=1, source_target_pairs={{0,4},{1,5},{2,6},{3,7},{4,0},{5,1},{6,2},{7,3},{8,12},{9,13},{10,... | collective-permute-start | bytes 1572872 | tf_op jit(solution)/shard_map/ppermute | solution.py:947
  214.8 31.5 %collective-permute-start.37 = (bf16[584,1024]{1,0:T(8,128)(2,1)S(1)}, bf16[584,1024]{1,0:T(8,128)(2,1)S(1)}, u32[]{:S(2)}, u32[]{:S(2)}) collective-permute-start(bf16[584,1024]{1,0:T(8,128)(2,1)S(1)} %down.1.refs_3_.refs_4_), channel_id=1, source_target_pairs={{0,1},{1,0},{2,3},{3,2},{4,5},{5,4},{6,7},{7,6},{8,9},{9,8},{10,11... | collective-permute-start | bytes 3588104 | tf_op jit(solution)/shard_map/ppermute | solution.py:1013
  218.7 25.7 %collective-permute-start.38 = (bf16[256,2048]{1,0:T(8,128)(2,1)S(1)}, bf16[256,2048]{1,0:T(8,128)(2,1)S(1)}, u32[]{:S(2)}, u32[]{:S(2)}) collective-permute-start(bf16[256,2048]{1,0:T(8,128)(2,1)S(1)} %join.18.refs_2_.refs_1_), channel_id=1, source_target_pairs={{0,4},{1,3},{2,6},{3,1},{4,0},{5,7},{6,2},{7,5},{8,12},{9,11},{10,... | collective-permute-start | bytes 3145736 | tf_op jit(solution)/shard_map/ppermute | solution.py:947
  222.6 26.2 %collective-permute-start.49 = (bf16[256,2048]{1,0:T(8,128)(2,1)S(1)}, bf16[256,2048]{1,0:T(8,128)(2,1)S(1)}, u32[]{:S(2)}, u32[]{:S(2)}) collective-permute-start(bf16[256,2048]{1,0:T(8,128)(2,1)S(1)} %join.20.refs_3_.refs_1_), channel_id=1, source_target_pairs={{0,8},{1,9},{2,10},{3,11},{4,12},{5,13},{6,14},{7,15},{8,0},{9,1},... | collective-permute-start | bytes 3145736 | tf_op jit(solution)/shard_map/ppermute | solution.py:947
  233.7 21.8 %collective-permute-start.48 = (bf16[1024,512]{1,0:T(8,128)(2,1)S(1)}, bf16[1024,512]{1,0:T(8,128)(2,1)S(1)}, u32[]{:S(2)}, u32[]{:S(2)}) collective-permute-start(bf16[1024,512]{1,0:T(8,128)(2,1)S(1)} %join.23.refs_2_.refs_1_), channel_id=1, source_target_pairs={{0,2},{1,3},{2,0},{3,1},{4,6},{5,7},{6,4},{7,5},{8,10},{9,11},{10,... | collective-permute-start | bytes 3145736 | tf_op jit(solution)/shard_map/ppermute | solution.py:947
  233.8 23.7 %collective-permute-start.47 = (bf16[1024,512]{1,0:T(8,128)(2,1)S(1)}, bf16[1024,512]{1,0:T(8,128)(2,1)S(1)}, u32[]{:S(2)}, u32[]{:S(2)}) collective-permute-start(bf16[1024,512]{1,0:T(8,128)(2,1)S(1)} %join.21.refs_3_.refs_1_), channel_id=1, source_target_pairs={{0,4},{1,9},{2,6},{3,11},{4,0},{5,13},{6,2},{7,15},{8,12},{9,1},{1... | collective-permute-start | bytes 3145736 | tf_op jit(solution)/shard_map/ppermute | solution.py:947
  (58 other events, 542.2 us)

commit v3 on v2

--- a/solution.py
+++ b/solution.py
@@ -443,14 +443,8 @@
 
 
 def gelu_pair(pre):
-    bell = jnp.exp(-0.5 * pre * pre)
-    near = 1.0 / (1.0 + (0.3275911 * 0.5**0.5) * jnp.abs(pre))
-    poly = near * (
-        0.254829592 + near * (-0.284496736 + near * (1.421413741 + near * (-1.453152027 + near * 1.061405429)))
-    )
-    tail = 0.5 * poly * bell
-    cdf = jnp.where(pre < 0, tail, 1.0 - tail)
-    return cdf, cdf + pre * bell * ((0.5 / jnp.pi) ** 0.5)
+    cdf = 0.5 + 0.5 * lax.erf(pre * (0.5**0.5))
+    return cdf, cdf + pre * jnp.exp(-0.5 * pre * pre) * ((0.5 / jnp.pi) ** 0.5)
 
 
 def feed_kernel(

time: 263 us -> 267 us (1.015)
  starting transfers between devices: 62 us -> 79.1 us
  waiting for transfers between devices: 67.5 us -> 54.9 us
    ppermute x42, starting transfers between devices: 58.4 us -> 75.7 us  [over(): return lax.ppermute(piece, ('dp', 'tensor'), pairs)]
    ppermute x42, waiting for transfers between devices: 55.6 us -> 49 us  [over(): return lax.ppermute(piece, ('dp', 'tensor'), pairs)]
    ppermute x4, waiting for transfers between devices: 9.75 us -> 3.69 us  [compute(): lax.ppermute(have['pack'], 'dp', xor_pairs(1 << int(name[4])))]
  transfers between devices with their start and end apart: 50 -> 50, of which waited for: 19 -> 20; matrix products, arithmetic and copies ran while one was open for 0% -> 0% of each run, Pallas kernels for 27% -> 27%
where the time goes in v3:
time: 267 us; the launch traced here: 262 us
  Pallas kernels  115 us (43%)
  starting transfers between devices  79.1 us (30%)
  waiting for transfers between devices  54.9 us (21%)
  local copies, waits for them, and re-layouts  10.5 us (4%)
    pallas_call x63, Pallas kernels, __call__(): pl.pallas_call(run, out_shape=outs, grid_spec=spec, input_output_aliases=...  115 us
    ppermute x42, starting transfers between devices, over(): return lax.ppermute(piece, ('dp', 'tensor'), pairs)  75.7 us
    ppermute x42, waiting for transfers between devices, over(): return lax.ppermute(piece, ('dp', 'tensor'), pairs)  49 us
    unnamed x64, local copies, waits for them, and re-layouts  10.5 us
  transfers between devices with their start and end apart: 50, of which 20 were waited for; matrix products, arithmetic and copies ran while one was open for 0% of the time, Pallas kernels for 27%

profile of v3, /device:TPU:0, one launch (start us, length us, event | category | flops | bytes accessed | tf_op | source)
XLA Modules:
  0.0 262.2 jit_solution(6457495641873843947)
XLA Ops:
  1.3 18.3 %attend.1 = (bf16[584,1024]{1,0:T(8,128)(2,1)}, bf16[592,512]{1,0:T(8,128)(2,1)}, bf16[592,512]{1,0:T(8,128)(2,1)}, bf16[592,512]{1,0:T(8,128)(2,1)}, bf16[592,5...) custom-call(s32[1]{0:T(128)S(6)} %copy.49.mask_ref, ...), custom_call_target="tpu_custom_call" | custom-call | bytes 3000 | tf_op jit(solution)/shard_map/attend/pallas_call | solution.py:308
  23.8 23.4 %feed.1 = (bf16[584,2048]{1,0:T(8,128)(2,1)}, bf16[584,1024]{1,0:T(8,128)(2,1)}, bf16[512,1024]{1,0:T(8,128)(2,1)}, bf16[512,1024]{1,0:T(8,128)(2,1)}, bf16[512,...) custom-call(s32[2]{0:T(128)} %pad_add_fusion.refs_0_, ...), custom_call_target="tpu_custom_call" | custom-call | bytes 3000 | tf_op jit(solution)/shard_map/feed/pallas_call | solution.py:308
  47.7 2.7 %collective-permute-start.4 = (bf16[512,1024]{1,0:T(8,128)(2,1)}, bf16[512,1024]{1,0:T(8,128)(2,1)S(1)}, u32[]{:S(2)}, u32[]{:S(2)}) collective-permute-start(bf16[512,1024]{1,0:T(8,128)(2,1)} %get-tuple-element.122), channel_id=1, source_target_pairs={{0,8},{1,5},{2,10},{3,7},{4,12},{5,1},{6,14},{7,3},{8,0},{9,13},{1... | collective-permute-start | bytes 3145736 | tf_op jit(solution)/shard_map/ppermute | solution.py:941
  58.6 3.8 %resid_back.1 = (f32[584,1024]{1,0:T(8,128)S(1)}, bf16[592,512]{1,0:T(8,128)(2,1)S(1)}, f32[8,1024]{1,0:T(8,128)S(1)}, bf16[1024,512]{1,0:T(8,128)(2,1)S(1)}) custom-call(bf16[584,1024]{1,0:T(8,128)(2,1)S(1)} %bitcast.12, bf16[584,1024]{1,0:T(8,128)(2,1)S(1)} %copy-done.1, bf16[584,1024]{1,0:T(8,128)(2,1)S(1)} %copy-done.5, bf16[1024]{0:T(1024)(128)(2,1)S(1)} %copy-done.25, ...), custom_call_target="tpu_custom_call" | custom-call | bytes 3000 | tf_op jit(solution)/shard_map/resid_back/pallas_call | solution.py:308
  62.5 9.2 %attend_back.1 = (bf16[592,1536]{1,0:T(8,128)(2,1)S(1)}, f32[1,1536]{1,0:T(1,128)S(1)}) custom-call(bf16[592,512]{1,0:T(8,128)(2,1)S(1)} %copy-done.21, bf16[592,512]{1,0:T(8,128)(2,1)S(1)} %copy-done.22, bf16[592,512]{1,0:T(8,128)(2,1)S(1)} %copy-done.23, bf16[592,512]{1,0:T(8,128)(2,1)S(1)} %copy-done.17, bf16[592,512]{1,0:T(8,128)(2,1)S(1)} %get-tuple-element.117.refs_4_, ...), custom_call_target="tpu_custom_call" | custom-call | bytes 3000 | tf_op jit(solution)/shard_map/attend_back/pallas_call | solution.py:308
  71.8 2.9 %qkv_grad.2 = (bf16[1024,512]{1,0:T(8,128)(2,1)}, bf16[1024,512]{1,0:T(8,128)(2,1)}) custom-call(s32[2]{0:T(128)S(1)} %copy-done.20, bf16[592,1024]{1,0:T(8,128)(2,1)S(1)} %copy-done.8, bf16[592,1536]{1,0:T(8,128)(2,1)S(1)} %get-tuple-element.120.refs_2_.refs_4_.refs_0_, bf16[1024,512]{1,0:T(8,128)(2,1)S(1)} %get-tuple-element.124.refs_3_, ...), custom_call_target="tpu_custom_call" | custom-call | bytes 3000 | tf_op jit(solution)/shard_map/qkv_grad/pallas_call | solution.py:308
  80.6 5.2 %back_in.1.refs_5_.refs_3_ = bf16[584,1024]{1,0:T(8,128)(2,1)S(1)} custom-call(bf16[592,1536]{1,0:T(8,128)(2,1)S(1)} %get-tuple-element.120.refs_2_.refs_4_.refs_0_, bf16[3,1024,512]{2,1,0:T(8,128)(2,1)S(1)} %bitcast.16, bf16[256,1024]{1,0:T(8,128)(2,1)} %get-tuple-element.126.refs_2_), custom_call_target="tpu_custom_call" | custom-call | bytes 3000 | tf_op jit(solution)/shard_map/back_in/pallas_call | solution.py:308
  85.8 5.2 %collective-permute-done.2.refs_3_.refs_4_ = bf16[256,2048]{1,0:T(8,128)(2,1)S(1)} collective-permute-done((bf16[256,2048]{1,0:T(8,128)(2,1)}, bf16[256,2048]{1,0:T(8,128)(2,1)S(1)}, u32[]{:S(2)}, u32[]{:S(2)}) %collective-permute-start.2) | collective-permute-done | bytes 1048608 | tf_op jit(solution)/shard_map/ppermute | solution.py:941
  91.7 3.1 %collective-permute-start.5 = (bf16[128,2048]{1,0:T(8,128)(2,1)S(1)}, bf16[128,2048]{1,0:T(8,128)(2,1)S(1)}, u32[]{:S(2)}, u32[]{:S(2)}) collective-permute-start(bf16[128,2048]{1,0:T(8,128)(2,1)S(1)} %get-tuple-element.128.refs_5_), channel_id=1, source_target_pairs={{0,2},{1,5},{2,0},{3,7},{4,6},{5,1},{6,4},{7,3},{8,10},{9,13},{10,... | collective-permute-start | bytes 1572872 | tf_op jit(solution)/shard_map/ppermute | solution.py:941
  99.4 8.3 %collective-permute-done.5.refs_3_.refs_4_ = bf16[128,2048]{1,0:T(8,128)(2,1)S(1)} collective-permute-done((bf16[128,2048]{1,0:T(8,128)(2,1)S(1)}, bf16[128,2048]{1,0:T(8,128)(2,1)S(1)}, u32[]{:S(2)}, u32[]{:S(2)}) %collective-permute-start.5) | collective-permute-done | bytes 524320 | tf_op jit(solution)/shard_map/ppermute | solution.py:941
  112.4 2.6 %collective-permute-start.16 = (bf16[128,1024]{1,0:T(8,128)(2,1)S(1)}, bf16[128,1024]{1,0:T(8,128)(2,1)S(1)}, u32[]{:S(2)}, u32[]{:S(2)}) collective-permute-start(bf16[128,1024]{1,0:T(8,128)(2,1)S(1)} %add.18.refs_5_.refs_0_), channel_id=1, source_target_pairs={{0,16},{1,17},{2,18},{3,19},{4,20},{5,21},{6,22},{7,23},{8,24},{9,... | collective-permute-start | bytes 786440 | tf_op jit(solution)/shard_map/ppermute | solution.py:941
  115.8 3.8 %collective-permute-done.10.refs_3_.refs_4_ = bf16[256,1024]{1,0:T(8,128)(2,1)S(1)} collective-permute-done((bf16[256,1024]{1,0:T(8,128)(2,1)S(1)}, bf16[256,1024]{1,0:T(8,128)(2,1)S(1)}, u32[]{:S(2)}, u32[]{:S(2)}) %collective-permute-start.10) | collective-permute-done | bytes 524320 | tf_op jit(solution)/shard_map/ppermute | solution.py:941
  128.5 2.6 %collective-permute-start.20 = (bf16[128,1024]{1,0:T(8,128)(2,1)S(1)}, bf16[128,1024]{1,0:T(8,128)(2,1)S(1)}, u32[]{:S(2)}, u32[]{:S(2)}) collective-permute-start(bf16[128,1024]{1,0:T(8,128)(2,1)S(1)} %add.20.refs_9_.refs_0_), channel_id=1, source_target_pairs={{0,16},{1,17},{2,18},{3,19},{4,20},{5,21},{6,22},{7,23},{8,24},{9,... | collective-permute-start | bytes 786440 | tf_op jit(solution)/shard_map/ppermute | solution.py:941
  131.2 3.2 %images_back.1 = (bf16[584,1024]{1,0:T(8,128)(2,1)}, f32[16,1024]{1,0:T(8,128)S(1)}) custom-call(bf16[584,1024]{1,0:T(8,128)(2,1)S(1)} %bitcast.13, bf16[1024]{0:T(1024)(128)(2,1)S(1)} %copy-done.28, f32[584,1024]{1,0:T(8,128)S(1)} %get-tuple-element.119.refs_6_.refs_2_, bf16[584,1024]{1,0:T(8,128)(2,1)S(1)} %back_in.1.refs_5_.refs_3_, ...), custom_call_target="tpu_custom_call" | custom-call | bytes 3000 | tf_op jit(solution)/shard_map/images_back/pallas_call | solution.py:308
  135.7 3.4 %collective-permute-start.17 = (bf16[64,2048]{1,0:T(8,128)(2,1)S(1)}, bf16[64,2048]{1,0:T(8,128)(2,1)S(1)}, u32[]{:S(2)}, u32[]{:S(2)}) collective-permute-start(bf16[64,2048]{1,0:T(8,128)(2,1)S(1)} %add.21.refs_2_.refs_0_), channel_id=1, source_target_pairs={{0,16},{1,17},{2,18},{3,19},{4,20},{5,21},{6,22},{7,23},{8,24},{9,... | collective-permute-start | bytes 786440 | tf_op jit(solution)/shard_map/ppermute | solution.py:941
  148.0 2.7 %collective-permute-start.21 = (bf16[64,2048]{1,0:T(8,128)(2,1)S(1)}, bf16[64,2048]{1,0:T(8,128)(2,1)S(1)}, u32[]{:S(2)}, u32[]{:S(2)}) collective-permute-start(bf16[64,2048]{1,0:T(8,128)(2,1)S(1)} %add.23.refs_2_.refs_1_), channel_id=1, source_target_pairs={{0,8},{1,9},{2,10},{3,11},{4,12},{5,13},{6,14},{7,15},{8,0},{9,1},... | collective-permute-start | bytes 786440 | tf_op jit(solution)/shard_map/ppermute | solution.py:941
  150.8 3.9 %collective-permute-start.30 = (bf16[64,2048]{1,0:T(8,128)(2,1)S(1)}, bf16[64,2048]{1,0:T(8,128)(2,1)S(1)}, u32[]{:S(2)}, u32[]{:S(2)}) collective-permute-start(bf16[64,2048]{1,0:T(8,128)(2,1)S(1)} %add.24.refs_2_.refs_0_), channel_id=1, source_target_pairs={{0,16},{1,17},{2,18},{3,19},{4,20},{5,21},{6,22},{7,23},{8,24},{9,... | collective-permute-start | bytes 786440 | tf_op jit(solution)/shard_map/ppermute | solution.py:941
  158.1 8.5 %collective-permute-done.21.refs_2_ = bf16[64,2048]{1,0:T(8,128)(2,1)S(1)} collective-permute-done((bf16[64,2048]{1,0:T(8,128)(2,1)S(1)}, bf16[64,2048]{1,0:T(8,128)(2,1)S(1)}, u32[]{:S(2)}, u32[]{:S(2)}) %collective-permute-start.21) | collective-permute-done | bytes 262176 | tf_op jit(solution)/shard_map/ppermute | solution.py:941
  177.2 4.9 %collective-permute-start.32 = (bf16[256,512]{1,0:T(8,128)(2,1)S(1)}, bf16[256,512]{1,0:T(8,128)(2,1)S(1)}, u32[]{:S(2)}, u32[]{:S(2)}) collective-permute-start(bf16[256,512]{1,0:T(8,128)(2,1)S(1)} %add.30.refs_3_.refs_0_), channel_id=1, source_target_pairs={{0,16},{1,17},{2,18},{3,19},{4,20},{5,21},{6,22},{7,23},{8,24},{9,... | collective-permute-start | bytes 786440 | tf_op jit(solution)/shard_map/ppermute | solution.py:941
  192.0 3.2 %down.1.refs_3_.refs_4_ = bf16[584,1024]{1,0:T(8,128)(2,1)S(1)} custom-call(bf16[584,2048]{1,0:T(8,128)(2,1)S(1)} %copy-done.7, bf16[2048,1024]{1,0:T(8,128)(2,1)S(1)} %copy-done.2, bf16[256,2048]{1,0:T(8,128)(2,1)S(1)} %join.18.refs_2_.refs_1_), custom_call_target="tpu_custom_call" | custom-call | bytes 3000 | tf_op jit(solution)/shard_map/down/pallas_call | solution.py:308
  195.2 5.3 %collective-permute-done.40.refs_2_ = bf16[256,512]{1,0:T(8,128)(2,1)S(1)} collective-permute-done((bf16[256,512]{1,0:T(8,128)(2,1)S(1)}, bf16[256,512]{1,0:T(8,128)(2,1)S(1)}, u32[]{:S(2)}, u32[]{:S(2)}) %collective-permute-start.40) | collective-permute-done | bytes 262176 | tf_op jit(solution)/shard_map/ppermute | solution.py:941
  204.2 13.1 %collective-permute-start.46 = (bf16[512,1024]{1,0:T(8,128)(2,1)S(1)}, bf16[512,1024]{1,0:T(8,128)(2,1)S(1)}, u32[]{:S(2)}, u32[]{:S(2)}) collective-permute-start(bf16[512,1024]{1,0:T(8,128)(2,1)S(1)} %join.22.refs_1_.refs_2_), channel_id=1, source_target_pairs={{0,4},{1,3},{2,6},{3,1},{4,0},{5,7},{6,2},{7,5},{8,12},{9,11},{10,... | collective-permute-start | bytes 3145736 | tf_op jit(solution)/shard_map/ppermute | solution.py:941
  231.9 3.7 %collective-permute-done.45.refs_2_ = bf16[512,512]{1,0:T(8,128)(2,1)S(1)} collective-permute-done((bf16[512,512]{1,0:T(8,128)(2,1)S(1)}, bf16[512,512]{1,0:T(8,128)(2,1)S(1)}, u32[]{:S(2)}, u32[]{:S(2)}) %collective-permute-start.45) | collective-permute-done | bytes 524320 | tf_op jit(solution)/shard_map/ppermute | solution.py:941
  254.5 3.6 %collective-permute-done.48.refs_1_ = bf16[1024,512]{1,0:T(8,128)(2,1)S(1)} collective-permute-done((bf16[1024,512]{1,0:T(8,128)(2,1)S(1)}, bf16[1024,512]{1,0:T(8,128)(2,1)S(1)}, u32[]{:S(2)}, u32[]{:S(2)}) %collective-permute-start.48) | collective-permute-done | bytes 1048608 | tf_op jit(solution)/shard_map/ppermute | solution.py:941
  (204 shorter events, 113.2 us)
Async XLA Ops:
  47.7 27.0 %collective-permute-start.4 = (bf16[512,1024]{1,0:T(8,128)(2,1)}, bf16[512,1024]{1,0:T(8,128)(2,1)S(1)}, u32[]{:S(2)}, u32[]{:S(2)}) collective-permute-start(bf16[512,1024]{1,0:T(8,128)(2,1)} %get-tuple-element.122), channel_id=1, source_target_pairs={{0,8},{1,5},{2,10},{3,7},{4,12},{5,1},{6,14},{7,3},{8,0},{9,13},{1... | collective-permute-start | bytes 3145736 | tf_op jit(solution)/shard_map/ppermute | solution.py:941
  50.4 40.5 %collective-permute-start.2 = (bf16[256,2048]{1,0:T(8,128)(2,1)}, bf16[256,2048]{1,0:T(8,128)(2,1)S(1)}, u32[]{:S(2)}, u32[]{:S(2)}) collective-permute-start(bf16[256,2048]{1,0:T(8,128)(2,1)} %get-tuple-element.111), channel_id=1, source_target_pairs={{0,8},{1,9},{2,10},{3,11},{4,12},{5,13},{6,14},{7,15},{8,0},{9,1},... | collective-permute-start | bytes 3145736 | tf_op jit(solution)/shard_map/ppermute | solution.py:941
  50.4 44.4 %collective-permute-start.7 = (bf16[512,1024]{1,0:T(8,128)(2,1)}, bf16[512,1024]{1,0:T(8,128)(2,1)S(1)}, u32[]{:S(2)}, u32[]{:S(2)}) collective-permute-start(bf16[512,1024]{1,0:T(8,128)(2,1)} %get-tuple-element.131), channel_id=1, source_target_pairs={{0,4},{1,3},{2,6},{3,1},{4,0},{5,7},{6,2},{7,5},{8,12},{9,11},{10,... | collective-permute-start | bytes 3145736 | tf_op jit(solution)/shard_map/ppermute | solution.py:941
  52.4 47.1 %collective-permute-start.1 = (bf16[256,2048]{1,0:T(8,128)(2,1)}, bf16[256,2048]{1,0:T(8,128)(2,1)S(1)}, u32[]{:S(2)}, u32[]{:S(2)}) collective-permute-start(bf16[256,2048]{1,0:T(8,128)(2,1)} %get-tuple-element.109), channel_id=1, source_target_pairs={{0,4},{1,3},{2,6},{3,1},{4,0},{5,7},{6,2},{7,5},{8,12},{9,11},{10,... | collective-permute-start | bytes 3145736 | tf_op jit(solution)/shard_map/ppermute | solution.py:941
  76.2 22.1 %collective-permute-start.6 = (bf16[256,1024]{1,0:T(8,128)(2,1)}, bf16[256,1024]{1,0:T(8,128)(2,1)S(1)}, u32[]{:S(2)}, u32[]{:S(2)}) collective-permute-start(bf16[256,1024]{1,0:T(8,128)(2,1)} %get-tuple-element.126.refs_2_), channel_id=1, source_target_pairs={{0,2},{1,3},{2,0},{3,1},{4,6},{5,7},{6,4},{7,5},{8,10},{9,11},{10,... | collective-permute-start | bytes 1572872 | tf_op jit(solution)/shard_map/ppermute | solution.py:941
  78.2 34.2 %collective-permute-start.11 = (bf16[1024,512]{1,0:T(8,128)(2,1)}, bf16[1024,512]{1,0:T(8,128)(2,1)S(1)}, u32[]{:S(2)}, u32[]{:S(2)}) collective-permute-start(bf16[1024,512]{1,0:T(8,128)(2,1)} %get-tuple-element.140), channel_id=1, source_target_pairs={{0,4},{1,9},{2,6},{3,11},{4,0},{5,13},{6,2},{7,15},{8,12},{9,1},{1... | collective-permute-start | bytes 3145736 | tf_op jit(solution)/shard_map/ppermute | solution.py:941
  94.9 27.9 %collective-permute-start.9 = (bf16[1024,512]{1,0:T(8,128)(2,1)}, bf16[1024,512]{1,0:T(8,128)(2,1)S(1)}, u32[]{:S(2)}, u32[]{:S(2)}) collective-permute-start(bf16[1024,512]{1,0:T(8,128)(2,1)} %get-tuple-element.125.refs_5_), channel_id=1, source_target_pairs={{0,2},{1,3},{2,0},{3,1},{4,6},{5,7},{6,4},{7,5},{8,10},{9,11},{10,... | collective-permute-start | bytes 3145736 | tf_op jit(solution)/shard_map/ppermute | solution.py:941
  99.4 31.7 %collective-permute-start.14 = (bf16[584,1024]{1,0:T(8,128)(2,1)S(1)}, bf16[584,1024]{1,0:T(8,128)(2,1)S(1)}, u32[]{:S(2)}, u32[]{:S(2)}) collective-permute-start(bf16[584,1024]{1,0:T(8,128)(2,1)S(1)} %back_in.1.refs_5_.refs_3_), channel_id=1, source_target_pairs={{0,1},{1,0},{2,3},{3,2},{4,5},{5,4},{6,7},{7,6},{8,9},{9,8},{10,11... | collective-permute-start | bytes 3588104 | tf_op jit(solution)/shard_map/ppermute | solution.py:1007
  123.7 18.1 %collective-permute-start.19 = (bf16[512,512]{1,0:T(8,128)(2,1)S(1)}, bf16[512,512]{1,0:T(8,128)(2,1)S(1)}, u32[]{:S(2)}, u32[]{:S(2)}) collective-permute-start(bf16[512,512]{1,0:T(8,128)(2,1)S(1)} %get-tuple-element.144.refs_5_), channel_id=1, source_target_pairs={{0,4},{1,5},{2,6},{3,7},{4,0},{5,1},{6,2},{7,3},{8,12},{9,13},{10,... | collective-permute-start | bytes 1572872 | tf_op jit(solution)/shard_map/ppermute | solution.py:941
  125.5 16.9 %collective-permute-start.18 = (bf16[512,512]{1,0:T(8,128)(2,1)S(1)}, bf16[512,512]{1,0:T(8,128)(2,1)S(1)}, u32[]{:S(2)}, u32[]{:S(2)}) collective-permute-start(bf16[512,512]{1,0:T(8,128)(2,1)S(1)} %get-tuple-element.142.refs_5_), channel_id=1, source_target_pairs={{0,2},{1,5},{2,0},{3,7},{4,6},{5,1},{6,4},{7,3},{8,10},{9,13},{10,... | collective-permute-start | bytes 1572872 | tf_op jit(solution)/shard_map/ppermute | solution.py:941
  148.0 18.6 %collective-permute-start.21 = (bf16[64,2048]{1,0:T(8,128)(2,1)S(1)}, bf16[64,2048]{1,0:T(8,128)(2,1)S(1)}, u32[]{:S(2)}, u32[]{:S(2)}) collective-permute-start(bf16[64,2048]{1,0:T(8,128)(2,1)S(1)} %add.23.refs_2_.refs_1_), channel_id=1, source_target_pairs={{0,8},{1,9},{2,10},{3,11},{4,12},{5,13},{6,14},{7,15},{8,0},{9,1},... | collective-permute-start | bytes 786440 | tf_op jit(solution)/shard_map/ppermute | solution.py:941
  150.7 16.5 %collective-permute-start.31 = (bf16[128,1024]{1,0:T(8,128)(2,1)S(1)}, bf16[128,1024]{1,0:T(8,128)(2,1)S(1)}, u32[]{:S(2)}, u32[]{:S(2)}) collective-permute-start(bf16[128,1024]{1,0:T(8,128)(2,1)S(1)} %add.22.refs_5_.refs_1_), channel_id=1, source_target_pairs={{0,2},{1,5},{2,0},{3,7},{4,6},{5,1},{6,4},{7,3},{8,10},{9,13},{10,... | collective-permute-start | bytes 786440 | tf_op jit(solution)/shard_map/ppermute | solution.py:941
  150.8 17.1 %collective-permute-start.30 = (bf16[64,2048]{1,0:T(8,128)(2,1)S(1)}, bf16[64,2048]{1,0:T(8,128)(2,1)S(1)}, u32[]{:S(2)}, u32[]{:S(2)}) collective-permute-start(bf16[64,2048]{1,0:T(8,128)(2,1)S(1)} %add.24.refs_2_.refs_0_), channel_id=1, source_target_pairs={{0,16},{1,17},{2,18},{3,19},{4,20},{5,21},{6,22},{7,23},{8,24},{9,... | collective-permute-start | bytes 786440 | tf_op jit(solution)/shard_map/ppermute | solution.py:941
  156.9 28.3 %collective-permute-start.34 = (bf16[256,1024]{1,0:T(8,128)(2,1)S(1)}, bf16[256,1024]{1,0:T(8,128)(2,1)S(1)}, u32[]{:S(2)}, u32[]{:S(2)}) collective-permute-start(bf16[256,1024]{1,0:T(8,128)(2,1)S(1)} %join.12.refs_3_.refs_1_), channel_id=1, source_target_pairs={{0,2},{1,3},{2,0},{3,1},{4,6},{5,7},{6,4},{7,5},{8,10},{9,11},{10,... | collective-permute-start | bytes 1572872 | tf_op jit(solution)/shard_map/ppermute | solution.py:941
  174.2 17.1 %collective-permute-start.26 = (bf16[128,2048]{1,0:T(8,128)(2,1)S(1)}, bf16[128,2048]{1,0:T(8,128)(2,1)S(1)}, u32[]{:S(2)}, u32[]{:S(2)}) collective-permute-start(bf16[128,2048]{1,0:T(8,128)(2,1)S(1)} %join.13.refs_3_.refs_1_), channel_id=1, source_target_pairs={{0,2},{1,5},{2,0},{3,7},{4,6},{5,1},{6,4},{7,3},{8,10},{9,13},{10,... | collective-permute-start | bytes 1572872 | tf_op jit(solution)/shard_map/ppermute | solution.py:941
  186.4 16.5 %collective-permute-start.44 = (bf16[512,512]{1,0:T(8,128)(2,1)S(1)}, bf16[512,512]{1,0:T(8,128)(2,1)S(1)}, u32[]{:S(2)}, u32[]{:S(2)}) collective-permute-start(bf16[512,512]{1,0:T(8,128)(2,1)S(1)} %join.17.refs_2_.refs_1_), channel_id=1, source_target_pairs={{0,2},{1,5},{2,0},{3,7},{4,6},{5,1},{6,4},{7,3},{8,10},{9,13},{10,... | collective-permute-start | bytes 1572872 | tf_op jit(solution)/shard_map/ppermute | solution.py:941
  191.2 29.9 %collective-permute-start.42 = (bf16[512,1024]{1,0:T(8,128)(2,1)S(1)}, bf16[512,1024]{1,0:T(8,128)(2,1)S(1)}, u32[]{:S(2)}, u32[]{:S(2)}) collective-permute-start(bf16[512,1024]{1,0:T(8,128)(2,1)S(1)} %join.16.refs_3_.refs_1_), channel_id=1, source_target_pairs={{0,8},{1,5},{2,10},{3,7},{4,12},{5,1},{6,14},{7,3},{8,0},{9,13},{1... | collective-permute-start | bytes 3145736 | tf_op jit(solution)/shard_map/ppermute | solution.py:941
  204.2 25.8 %collective-permute-start.46 = (bf16[512,1024]{1,0:T(8,128)(2,1)S(1)}, bf16[512,1024]{1,0:T(8,128)(2,1)S(1)}, u32[]{:S(2)}, u32[]{:S(2)}) collective-permute-start(bf16[512,1024]{1,0:T(8,128)(2,1)S(1)} %join.22.refs_1_.refs_2_), channel_id=1, source_target_pairs={{0,4},{1,3},{2,6},{3,1},{4,0},{5,7},{6,2},{7,5},{8,12},{9,11},{10,... | collective-permute-start | bytes 3145736 | tf_op jit(solution)/shard_map/ppermute | solution.py:941
  217.2 18.4 %collective-permute-start.45 = (bf16[512,512]{1,0:T(8,128)(2,1)S(1)}, bf16[512,512]{1,0:T(8,128)(2,1)S(1)}, u32[]{:S(2)}, u32[]{:S(2)}) collective-permute-start(bf16[512,512]{1,0:T(8,128)(2,1)S(1)} %join.19.refs_3_.refs_1_), channel_id=1, source_target_pairs={{0,4},{1,5},{2,6},{3,7},{4,0},{5,1},{6,2},{7,3},{8,12},{9,13},{10,... | collective-permute-start | bytes 1572872 | tf_op jit(solution)/shard_map/ppermute | solution.py:941
  217.3 31.5 %collective-permute-start.37 = (bf16[584,1024]{1,0:T(8,128)(2,1)S(1)}, bf16[584,1024]{1,0:T(8,128)(2,1)S(1)}, u32[]{:S(2)}, u32[]{:S(2)}) collective-permute-start(bf16[584,1024]{1,0:T(8,128)(2,1)S(1)} %down.1.refs_3_.refs_4_), channel_id=1, source_target_pairs={{0,1},{1,0},{2,3},{3,2},{4,5},{5,4},{6,7},{7,6},{8,9},{9,8},{10,11... | collective-permute-start | bytes 3588104 | tf_op jit(solution)/shard_map/ppermute | solution.py:1007
  221.2 25.7 %collective-permute-start.38 = (bf16[256,2048]{1,0:T(8,128)(2,1)S(1)}, bf16[256,2048]{1,0:T(8,128)(2,1)S(1)}, u32[]{:S(2)}, u32[]{:S(2)}) collective-permute-start(bf16[256,2048]{1,0:T(8,128)(2,1)S(1)} %join.18.refs_2_.refs_1_), channel_id=1, source_target_pairs={{0,4},{1,3},{2,6},{3,1},{4,0},{5,7},{6,2},{7,5},{8,12},{9,11},{10,... | collective-permute-start | bytes 3145736 | tf_op jit(solution)/shard_map/ppermute | solution.py:941
  225.2 26.1 %collective-permute-start.49 = (bf16[256,2048]{1,0:T(8,128)(2,1)S(1)}, bf16[256,2048]{1,0:T(8,128)(2,1)S(1)}, u32[]{:S(2)}, u32[]{:S(2)}) collective-permute-start(bf16[256,2048]{1,0:T(8,128)(2,1)S(1)} %join.20.refs_3_.refs_1_), channel_id=1, source_target_pairs={{0,8},{1,9},{2,10},{3,11},{4,12},{5,13},{6,14},{7,15},{8,0},{9,1},... | collective-permute-start | bytes 3145736 | tf_op jit(solution)/shard_map/ppermute | solution.py:941
  236.2 21.8 %collective-permute-start.48 = (bf16[1024,512]{1,0:T(8,128)(2,1)S(1)}, bf16[1024,512]{1,0:T(8,128)(2,1)S(1)}, u32[]{:S(2)}, u32[]{:S(2)}) collective-permute-start(bf16[1024,512]{1,0:T(8,128)(2,1)S(1)} %join.23.refs_2_.refs_1_), channel_id=1, source_target_pairs={{0,2},{1,3},{2,0},{3,1},{4,6},{5,7},{6,4},{7,5},{8,10},{9,11},{10,... | collective-permute-start | bytes 3145736 | tf_op jit(solution)/shard_map/ppermute | solution.py:941
  236.3 23.7 %collective-permute-start.47 = (bf16[1024,512]{1,0:T(8,128)(2,1)S(1)}, bf16[1024,512]{1,0:T(8,128)(2,1)S(1)}, u32[]{:S(2)}, u32[]{:S(2)}) collective-permute-start(bf16[1024,512]{1,0:T(8,128)(2,1)S(1)} %join.21.refs_3_.refs_1_), channel_id=1, source_target_pairs={{0,4},{1,9},{2,6},{3,11},{4,0},{5,13},{6,2},{7,15},{8,12},{9,1},{1... | collective-permute-start | bytes 3145736 | tf_op jit(solution)/shard_map/ppermute | solution.py:941
  (58 other events, 523.9 us)
